TPU v7x, 32 devices: a whole 2x2x4 slice. The times are simulated.
32 devices in a mesh: groups: 2 (over y), gs: 16 (over z, x, core).
Axes of the slice: x: 2, y: 2, z: 4, core: 2. Of those that a mesh axis runs over, the one named last changes fastest.
Arguments:
- params: float32 [59, 131072], P(None, ('groups', 'gs')), parts along dimension 1, may hold values from -620 to 620, as said below
- requests: int32 [512, 256], P(('groups', 'gs')), parts along dimension 0, may hold values from 0 to 4095, as said below
- member: int32 [512, 256], P(('groups', 'gs')), parts along dimension 0, may hold values from 0 to 4095, as said below
- tile_len: int32 [512], P(('groups', 'gs')), parts along dimension 0, may hold values from 1 to 256, 32768 in all
- tile_pos: int32 [512], P(('groups', 'gs')), parts along dimension 0, may hold values from 0 to 32399, as said below
- cam_shift: float32 [3, 16], P(None, 'groups'), parts along dimension 1, may hold values from -20 to 20
- pixel_grad: float32 [512, 3, 256], P(('groups', 'gs')), parts along dimension 0, may hold values from -6 to 6
Outputs:
- image: float32 [512, 3, 256], P(('groups', 'gs')), parts along dimension 0
- grad_params: float32 [59, 131072], P(None, ('groups', 'gs')), parts along dimension 1
There are 2 independent parts, one for each index of `groups`. A program takes and returns all parts, laid end to end along the dimension named above; each array names one. Nothing has to cross between parts.
Inputs may be any that keep to these rules, and one draw needn't show every extreme that they name: `params`: rows 0 and 1 lie in -620 to 620, row 2 in 180 to 620, rows 3 to 5 in log 0.12 to log 0.9, row 6 in 1 to 2, rows 7 to 9 in -3 to 3, row 10 in -6 to 8, the rest in -1.5 to 1.5. `requests`: for each owner q, the rows r * 16 + q over all renderers r name each of its 4096 Gaussians exactly once. `member`: the 16 lists of one renderer name each of its 4096 slots exactly once. `tile_pos`: the tiles of one view are distinct.
All inputs are finite; a program needn't handle non-finite values. No bound on the sum of `tile_len` on one device may be relied on, other than what follows from the above.
Results may differ from a plain program's by a relative error of at most 0.0024.
Values sent between devices are 32-bit elements; how exact they have to be, the bound alone decides.
No kernel may reach another device: no remote copies, remote signals or barrier semaphores. Data moves between devices by JAX's collectives and lax.ppermute only.
A program may use at most 128 MiB of HBM per device.

v0:
```python
import functools

import jax
import jax.numpy as jnp
from jax import lax
from jax.experimental import pallas as pl
from jax.experimental.pallas import tpu as pltpu
from jax.sharding import PartitionSpec as P

f32, bf16, i32 = jnp.float32, jnp.bfloat16, jnp.int32

WIDE = 256
ATTRS = 9
SIDE = 16
ACROSS = 240
SCALE = 1920.0
LOG2E = 1.4426950408889634
FAR = -1.0e9

sh_c0 = 0.28209479177387814
sh_c1 = 0.4886025119029199
sh_c2 = (
    1.0925484305920792,
    -1.0925484305920792,
    0.31539156525252005,
    -1.0925484305920792,
    0.5462742152960396,
)
sh_c3 = (
    -0.5900435899266435,
    2.890611442640554,
    -0.4570457994644658,
    0.3731763325901154,
    -0.4570457994644658,
    1.445305721320277,
    -0.5900435899266435,
)


def project(table, shift):
    xpos = table[0] - shift[0]
    ypos = table[1] - shift[1]
    zpos = table[2] - shift[2]
    scales = [jnp.exp(table[3 + k]) for k in range(3)]
    quat = table[6:10]
    norm = 1.0 / jnp.sqrt(sum(part * part for part in quat))
    qw, qx, qy, qz = (part * norm for part in quat)
    rot = [
        [1 - 2 * (qy * qy + qz * qz), 2 * (qx * qy - qw * qz), 2 * (qx * qz + qw * qy)],
        [2 * (qx * qy + qw * qz), 1 - 2 * (qx * qx + qz * qz), 2 * (qy * qz - qw * qx)],
        [2 * (qx * qz - qw * qy), 2 * (qy * qz + qw * qx), 1 - 2 * (qx * qx + qy * qy)],
    ]
    inverse_z = 1.0 / zpos
    mean_u = xpos * inverse_z
    mean_v = ypos * inverse_z
    stretch = [scale * inverse_z for scale in scales]
    first = [(rot[0][k] - mean_u * rot[2][k]) * stretch[k] for k in range(3)]
    second = [(rot[1][k] - mean_v * rot[2][k]) * stretch[k] for k in range(3)]
    cov_a = first[0] * first[0] + first[1] * first[1] + first[2] * first[2] + 8e-08
    cov_b = first[0] * second[0] + first[1] * second[1] + first[2] * second[2]
    cov_c = second[0] * second[0] + second[1] * second[1] + second[2] * second[2] + 8e-08
    over_det = 1.0 / (cov_a * cov_c - cov_b * cov_b)
    over_length = 1.0 / jnp.sqrt(xpos * xpos + ypos * ypos + zpos * zpos)
    dx, dy, dz = (xpos * over_length, ypos * over_length, zpos * over_length)
    xx, yy, zz = (dx * dx, dy * dy, dz * dz)
    basis = [
        -sh_c1 * dy,
        sh_c1 * dz,
        -sh_c1 * dx,
        sh_c2[0] * dx * dy,
        sh_c2[1] * dy * dz,
        sh_c2[2] * (2 * zz - xx - yy),
        sh_c2[3] * dx * dz,
        sh_c2[4] * (xx - yy),
        sh_c3[0] * dy * (3 * xx - yy),
        sh_c3[1] * dx * dy * dz,
        sh_c3[2] * dy * (4 * zz - xx - yy),
        sh_c3[3] * dz * (2 * zz - 3 * xx - 3 * yy),
        sh_c3[4] * dx * (4 * zz - xx - yy),
        sh_c3[5] * dz * (xx - yy),
        sh_c3[6] * dx * (xx - 3 * yy),
    ]
    colors = []
    for k in range(3):
        total = 0.5 + sh_c0 * table[11 + 16 * k]
        for j, part in enumerate(basis):
            total = total + part * table[12 + 16 * k + j]
        colors.append(jnp.maximum(total, 0.0))
    opacity = 1.0 / (1.0 + jnp.exp(-table[10]))
    return [
        mean_u,
        mean_v,
        cov_c * over_det,
        -cov_b * over_det,
        cov_a * over_det,
        opacity,
        colors[0],
        colors[1],
        colors[2],
    ]


def pieces(value, count):
    out = []
    for left in range(count - 1, -1, -1):
        part = value.astype(bf16)
        out.append(part)
        if left:
            value = value - part.astype(f32)
    return out


def dot(one, other):
    return jnp.dot(one, other, preferred_element_type=f32)


def dot_nt(one, other):
    return lax.dot_general(one, other, (((1,), (1,)), ((), ())), preferred_element_type=f32)


def one_hot(low_row):
    rows = lax.broadcasted_iota(i32, (WIDE, WIDE), 0)
    return jnp.where(rows == low_row, 1.0, 0.0).astype(bf16)


def get(ref, start, count, stride=1, many=WIDE):
    rows = pl.ds(start, count, stride=stride) if stride > 1 else pl.ds(start, count)
    return jnp.concatenate([ref[h, rows, :] for h in range(many // 128)], axis=1)


def put(ref, start, count, value, stride=1):
    rows = pl.ds(start, count, stride=stride) if stride > 1 else pl.ds(start, count)
    for h in range(value.shape[1] // 128):
        ref[h, rows, :] = value[:, 128 * h : 128 * h + 128]


def invert(index_ref, inverse_ref):
    blocks = index_ref.shape[0]
    high_rows = lax.broadcasted_iota(i32, (blocks, WIDE), 0)
    lanes = lax.broadcasted_iota(i32, (blocks, WIDE), 1).astype(f32)
    total = jnp.zeros((2 * blocks, WIDE), f32)
    for j in range(blocks):
        row = index_ref[j : j + 1, :]
        here = high_rows == lax.shift_right_logical(row, 8)
        left = jnp.concatenate([jnp.where(here, float(j), 0.0), jnp.where(here, lanes, 0.0)], axis=0)
        total = total + dot_nt(left.astype(bf16), one_hot(row & (WIDE - 1)))
    found = total[:blocks] * float(WIDE) + total[blocks:]
    inverse_ref[...] = found.astype(i32)


def permute(held_ref, index_ref, count, give):
    blocks = index_ref.shape[0]
    parts = pieces(get(held_ref, 0, ATTRS * blocks), count)
    high_rows = lax.broadcasted_iota(i32, (blocks, WIDE), 0)
    for j in range(blocks):
        row = index_ref[j : j + 1, :]
        spread = one_hot(row & (WIDE - 1))
        high = lax.shift_right_logical(row, 8)
        found = dot(parts[0], spread)
        for part in parts[1:]:
            found = found + dot(part, spread)
        high_eight = jnp.broadcast_to(high, (8, WIDE))
        eight = found[0:8]
        for b in range(1, blocks):
            eight = jnp.where(high_eight == b, found[8 * b : 8 * b + 8], eight)
        ninth = jnp.sum(jnp.where(high_rows == high, found[8 * blocks :], 0.0), axis=0, keepdims=True)
        give(j, eight, ninth)


def put_travel(out_ref, blocks, packed, j, eight, ninth):
    for h in range(2):
        half = slice(128 * h, 128 * h + 128)
        if packed:
            out_ref[18 * j + 8 * h : 18 * j + 8 * h + 8, :] = eight[:, half]
            out_ref[18 * j + 16 + h : 18 * j + 17 + h, :] = ninth[:, half]
        else:
            out_ref[pl.ds(2 * j + h, 8, stride=2 * blocks), :] = eight[:, half]
            out_ref[16 * blocks + 2 * j + h : 16 * blocks + 2 * j + h + 1, :] = ninth[:, half]


def take_travel(in_ref, held_ref, blocks, packed):
    for j in range(blocks):
        for h in range(2):
            if packed:
                held_ref[h, 8 * j : 8 * j + 8, :] = in_ref[18 * j + 8 * h : 18 * j + 8 * h + 8, :]
                held_ref[h, 8 * blocks + j : 8 * blocks + j + 1, :] = in_ref[18 * j + 16 + h : 18 * j + 17 + h, :]
            else:
                held_ref[h, 8 * j : 8 * j + 8, :] = in_ref[pl.ds(2 * j + h, 8, stride=2 * blocks), :]
                held_ref[h, 8 * blocks + j : 8 * blocks + j + 1, :] = in_ref[
                    16 * blocks + 2 * j + h : 16 * blocks + 2 * j + h + 1, :
                ]


def prepare_kernel(params_ref, member_ref, grad_ref, dense_ref, inverse_ref, light_ref, turned_ref, light):
    width, count = params_ref.shape
    blocks = count // WIDE
    for first in range(0, width, 8):
        rows = min(8, width - first)
        for j in range(blocks):
            value = params_ref[first : first + rows, WIDE * j : WIDE * (j + 1)]
            put(dense_ref, first * blocks + j, rows, value, blocks)
    invert(member_ref, inverse_ref)
    tiles = grad_ref.shape[0]
    light[...] = jnp.zeros_like(light)
    for t in range(tiles):
        high, low = pieces(grad_ref[t], 2)
        light[16 * t : 16 * t + 3, :] = high.astype(f32)
        light[16 * t + 3 : 16 * t + 6, :] = low.astype(f32)
        light[16 * t + 6 : 16 * t + 9, :] = high.astype(f32)
    light_ref[...] = light[...].astype(bf16)
    for t in range(tiles):
        turned_ref[t] = light[16 * t : 16 * t + 16, :].T.astype(bf16)


def shifts(inverse, slots_per, cam_ref):
    views = cam_ref.shape[1]
    view = lax.rem(lax.div(inverse, slots_per), views)
    out = []
    for axis in range(3):
        value = jnp.full(inverse.shape, cam_ref[axis, 0], f32)
        for k in range(1, views):
            value = jnp.where(view == k, cam_ref[axis, k], value)
        out.append(value)
    return out


def dense_rows(ref, count, blocks):
    return [get(ref, k * blocks, blocks) for k in range(count)]


def owner_kernel(slots_per, packed, asked_ref, dense_ref, cam_ref, attrs_ref, inverse_ref, held):
    blocks = asked_ref.shape[0]
    width = dense_ref.shape[1] // blocks
    invert(asked_ref, inverse_ref)
    shift = shifts(inverse_ref[...], slots_per, cam_ref)
    attrs = project(dense_rows(dense_ref, width, blocks), shift)
    for a in range(8):
        put(held, a, blocks, attrs[a], 8)
    put(held, 8 * blocks, blocks, attrs[8])
    permute(held, asked_ref, 3, functools.partial(put_travel, attrs_ref, blocks, packed))


def return_kernel(slots_per, packed, back_ref, inverse_ref, dense_ref, cam_ref, out_ref, held, flat, grads):
    blocks = inverse_ref.shape[0]
    width = dense_ref.shape[1] // blocks
    take_travel(back_ref, held, blocks, packed)

    def give(j, eight, ninth):
        put(flat, j, 8, eight, blocks)
        put(flat, 8 * blocks + j, 1, ninth)

    permute(held, inverse_ref, 2, give)
    shift = shifts(inverse_ref[...], slots_per, cam_ref)
    _, back = jax.vjp(lambda rows: project(rows, shift), dense_rows(dense_ref, width, blocks))
    (rows,) = back(dense_rows(flat, ATTRS, blocks))
    for k in range(width):
        put(grads, k * blocks, blocks, rows[k])
    for first in range(0, width, 8):
        count = min(8, width - first)
        for j in range(blocks):
            value = get(grads, first * blocks + j, count, blocks)
            out_ref[first : first + count, WIDE * j : WIDE * (j + 1)] = value


def spread_scalars(values, tiles):
    rows = lax.broadcasted_iota(i32, (tiles, WIDE), 0)
    out = jnp.full((tiles, WIDE), values[0], values[0].dtype)
    for t in range(1, tiles):
        out = jnp.where(rows == t, values[t], out)
    return out


def offsets(index):
    column = lax.rem(index, SIDE).astype(f32) - (SIDE - 1) / 2
    row = lax.div(index, SIDE).astype(f32) - (SIDE - 1) / 2
    return column, row


def pick(index, choices):
    out = jnp.zeros(index.shape, f32)
    for k, choice in enumerate(choices):
        out = jnp.where(index == k, choice, out)
    return out


def render_kernel(
    packed,
    arrived_ref,
    member_ref,
    inverse_ref,
    light_ref,
    turned_ref,
    length_ref,
    place_ref,
    image_ref,
    back_ref,
    held,
    flat,
    coefs,
    sums,
    upper,
    lower,
    monomials,
    moments,
):
    tiles = member_ref.shape[0]
    blocks = tiles

    take_travel(arrived_ref, held, blocks, packed)

    def give(j, eight, ninth):
        put(flat, j, 8, eight, blocks)
        put(flat, 8 * blocks + j, 1, ninth)

    permute(held, member_ref, 3, give)

    mu, nu, con_a, con_b, con_c, opacity, *colors = dense_rows(flat, ATTRS, blocks)
    across = [lax.rem(place_ref[t], ACROSS).astype(f32) for t in range(tiles)]
    down = [lax.div(place_ref[t], ACROSS).astype(f32) for t in range(tiles)]
    centre_u = spread_scalars([(x * SIDE + SIDE / 2) / SCALE - 1.0 for x in across], tiles)
    centre_v = spread_scalars([(y * SIDE + SIDE / 2) / SCALE - 0.5625 for y in down], tiles)
    lengths = spread_scalars([length_ref[t] for t in range(tiles)], tiles)
    live = lax.broadcasted_iota(i32, (tiles, WIDE), 1) < lengths
    m = (mu - centre_u) * SCALE
    n = (nu - centre_v) * SCALE
    unit = LOG2E / (SCALE * SCALE)
    a = con_a * (-0.5 * unit)
    b = con_b * -unit
    c = con_c * (-0.5 * unit)
    lift = -2.0 * a * m - b * n
    tilt = -2.0 * c * n - b * m
    rest = -0.5 * (lift * m + tilt * n) + jnp.log2(opacity)
    terms = [a, b, c, lift, tilt]
    terms = [jnp.where(live, term, 0.0) for term in terms] + [jnp.where(live, rest, FAR)]
    coefs[...] = jnp.zeros_like(coefs)
    for k, term in enumerate(terms):
        for s, part in enumerate(pieces(term, 3)):
            row = 6 * s + k
            put(coefs, row * tiles, tiles, part.astype(f32))
    for k, color in enumerate(colors):
        high, low = (part.astype(f32) for part in pieces(color, 2))
        for row, part in ((32 + k, high), (35 + k, high), (38 + k, low)):
            put(coefs, row * tiles, tiles, part)

    row_index = lax.broadcasted_iota(i32, (WIDE, WIDE), 0)
    lane_index = lax.broadcasted_iota(i32, (WIDE, WIDE), 1)
    upper[...] = jnp.where(row_index < lane_index, 1.0, 0.0).astype(bf16)
    lower[...] = jnp.where(row_index > lane_index, 1.0, 0.0).astype(bf16)
    column, row = offsets(lax.broadcasted_iota(i32, (WIDE, 32), 0))
    which = lax.broadcasted_iota(i32, (WIDE, 32), 1)
    which = jnp.where(which < 18, lax.rem(which, 6), 6)
    one = jnp.ones((WIDE, 32), f32)
    monomials[...] = pick(
        which, [column * column, column * row, row * row, column, row, one]
    ).astype(bf16)
    column, row = offsets(lax.broadcasted_iota(i32, (16, WIDE), 1))
    which = lax.broadcasted_iota(i32, (16, WIDE), 0)
    one = jnp.ones((16, WIDE), f32)
    moments[...] = pick(
        which, [column * column, column * row, row * row, column, row, one]
    ).astype(bf16)
    sums[...] = jnp.zeros_like(sums)

    def one_tile(t, many):
        block = pl.ds(pl.multiple_of(16 * t, 16), 16)
        coef = get(coefs, t, 32, tiles, many).astype(bf16)
        color = get(coefs, t + 32 * tiles, 16, tiles, many).astype(bf16)
        power = jnp.exp2(dot(monomials[...], coef))
        alpha = jnp.minimum(power, 0.99)
        keep = 1.0 - alpha
        high, low = pieces(jnp.log2(keep), 2)
        before = upper[:many, :many]
        through = jnp.exp2(dot(high, before) + dot(low, before))
        weight = alpha * through
        high, low = pieces(weight, 2)
        picture = dot_nt(color, high) + dot_nt(color, low)
        image_ref[t] = picture[0:3] + picture[6:9]
        tint = dot(light_ref[block, :], high) + dot(light_ref[block, :], low)
        pull = dot(turned_ref[t], color)
        high, low = pieces(pull * weight, 2)
        after = lower[:many, :many]
        behind = dot(high, after) + dot(low, after)
        slope = (pull * through - behind / keep) * alpha
        high, low = pieces(jnp.where(power < 0.99, slope, 0.0), 2)
        moment = dot(moments[...], high) + dot(moments[...], low)
        put(sums, pl.multiple_of(16 * t, 16), 8, moment[0:8])
        put(sums, pl.multiple_of(16 * t + 8, 8), 8, tint[0:8] + pltpu.roll(tint[0:8], 5, 0))

    def step(t, carry):
        short = length_ref[t] <= WIDE // 2

        @pl.when(short)
        def _():
            one_tile(t, WIDE // 2)

        @pl.when(jnp.logical_not(short))
        def _():
            one_tile(t, WIDE)

        return carry

    lax.fori_loop(0, tiles, step, 0)

    m_xx, m_xy, m_yy, m_x, m_y, m_one = [get(sums, k, tiles, 16) for k in range(6)]
    d_x = m_x - m * m_one
    d_y = m_y - n * m_one
    d_xx = m_xx - m * (m_x + d_x)
    d_xy = m_xy - m * m_y - n * d_x
    d_yy = m_yy - n * (m_y + d_y)
    shrink = 1.0 / SCALE
    grads = [
        (con_a * d_x + con_b * d_y) * shrink,
        (con_c * d_y + con_b * d_x) * shrink,
        d_xx * (-0.5 * shrink * shrink),
        d_xy * (-shrink * shrink),
        d_yy * (-0.5 * shrink * shrink),
        m_one / opacity,
        *[get(sums, 8 + k, tiles, 16) for k in range(3)],
    ]
    for k in range(8):
        put(held, k, blocks, grads[k], 8)
    put(held, 8 * blocks, blocks, grads[8])
    permute(held, inverse_ref, 2, functools.partial(put_travel, back_ref, blocks, packed))


def vmem(count):
    return [pl.BlockSpec(memory_space=pltpu.VMEM)] * count


def smem(count):
    return [pl.BlockSpec(memory_space=pltpu.SMEM)] * count


def shape(*dims, dtype=f32):
    return jax.ShapeDtypeStruct(dims, dtype)


def call(kernel, name, ins, outs, scratch, cycles):
    return pl.pallas_call(
        kernel,
        out_shape=outs,
        in_specs=ins,
        out_specs=vmem(len(outs)),
        scratch_shapes=scratch,
        name=name,
        compiler_params=pltpu.CompilerParams(vmem_limit_bytes=48 * 1024 * 1024),
        cost_estimate=pl.CostEstimate(flops=cycles, bytes_accessed=4_000_000, transcendentals=0),
    )


def travel(rows, peers, slots, packed):
    total = rows.shape[0]
    if packed:
        parts = rows.reshape(peers, 1, -1)
    else:
        parts = jnp.swapaxes(rows.reshape(ATTRS, peers, slots), 0, 1)
    parts = lax.all_to_all(parts, "gs", split_axis=0, concat_axis=0, tiled=True)
    if not packed:
        parts = jnp.swapaxes(parts, 0, 1)
    return parts.reshape(total, 128)


def on_device(params, requests, member, tile_len, tile_pos, cam_shift, pixel_grad):
    peers, slots = requests.shape
    width, count = params.shape
    tiles = member.shape[0]
    blocks = count // WIDE
    packed = slots % WIDE == 0
    held = pltpu.VMEM((2, ATTRS * blocks, 128), f32)
    rows = shape(18 * blocks, 128)
    index = shape(blocks, WIDE, dtype=i32)

    asked = lax.all_to_all(requests, "gs", split_axis=0, concat_axis=0, tiled=True)
    asked = asked.reshape(blocks, WIDE)
    dense, inverse, light, turned = call(
        prepare_kernel,
        "prepare",
        vmem(3),
        [
            shape(2, width * blocks, 128),
            index,
            shape(16 * tiles, WIDE, dtype=bf16),
            shape(tiles, WIDE, 16, dtype=bf16),
        ],
        [pltpu.VMEM((16 * tiles, WIDE), f32)],
        10_000_000,
    )(params, member, pixel_grad)
    attrs, place = call(
        functools.partial(owner_kernel, slots, packed),
        "owner",
        vmem(2) + smem(1),
        [rows, index],
        [held],
        10_000_000,
    )(asked, dense, cam_shift)
    arrived = travel(attrs, peers, slots, packed)
    image, back = call(
        functools.partial(render_kernel, packed),
        "render",
        vmem(5) + smem(2),
        [shape(tiles, 3, WIDE), rows],
        [
            held,
            held,
            pltpu.VMEM((2, 48 * tiles, 128), f32),
            pltpu.VMEM((2, 16 * tiles, 128), f32),
            pltpu.VMEM((WIDE, WIDE), bf16),
            pltpu.VMEM((WIDE, WIDE), bf16),
            pltpu.VMEM((WIDE, 32), bf16),
            pltpu.VMEM((16, WIDE), bf16),
        ],
        100_000_000,
    )(arrived, member, inverse, light, turned, tile_len, tile_pos)
    returned = travel(back, peers, slots, packed)
    (grad_params,) = call(
        functools.partial(return_kernel, slots, packed),
        "return",
        vmem(3) + smem(1),
        [shape(width, count)],
        [held, held, pltpu.VMEM((2, width * blocks, 128), f32)],
        10_000_000,
    )(returned, place, dense, cam_shift)
    return (image, grad_params)


def solution(mesh):
    return jax.shard_map(
        on_device,
        mesh=mesh,
        in_specs=(
            P(None, ("groups", "gs")),
            P(("groups", "gs"), None),
            P(("groups", "gs"), None),
            P(("groups", "gs")),
            P(("groups", "gs")),
            P(None, "groups"),
            P(("groups", "gs"), None, None),
        ),
        out_specs=(P(("groups", "gs"), None, None), P(None, ("groups", "gs"))),
        check_vma=False,
    )
```

profile of v0, /device:TPU:0, one launch (start us, length us, event | category | flops | bytes accessed | tf_op | source)
XLA Modules:
  0.0 65.1 jit_solution(11268979030784988405)
XLA Ops:
  0.6 0.0 copy-start.5
  0.6 1.3 %all_to_all.13 = s32[16,1,256]{2,1,0:T(1,128)} reshape(s32[16,256]{1,0:T(8,128)} %param.8) | data formatting | bytes 32768 | tf_op jit(solution)/shard_map/all_to_all | solution.py:473
  2.0 7.4 %all-to-all-start = ((s32[16,1,256]{2,1,0:T(1,128)}), s32[16,1,256]{2,1,0:T(1,128)S(1)}, u32[]{:S(2)}, u32[]{:S(2)}) async-start(s32[16,1,256]{2,1,0:T(1,128)} %all_to_all.13), calls=%async_computation | async-start | bytes 32768 | tf_op jit(solution)/shard_map/all_to_all | solution.py:473
  9.4 0.0 copy-done.5
  9.4 0.0 copy-start.1
  9.4 0.7 %copy-done.1 = s32[16,256]{1,0:T(8,128)S(1)} copy-done((s32[16,256]{1,0:T(8,128)S(1)}, s32[16,256]{1,0:T(8,128)}, u32[]{:S(2)}) %copy-start.1) | copy-done | bytes 16408
  10.1 0.0 copy-start
  10.1 1.2 %copy-done = f32[59,4096]{1,0:T(8,128)S(1)} copy-done((f32[59,4096]{1,0:T(8,128)S(1)}, f32[59,4096]{1,0:T(8,128)}, u32[]{:S(2)}) %copy-start) | copy-done | bytes 966680
  11.3 1.1 %prepare.1 = (f32[2,944,128]{2,1,0:T(8,128)S(1)}, s32[16,256]{1,0:T(8,128)S(1)}, bf16[256,256]{1,0:T(8,128)(2,1)S(1)}, bf16[16,256,16]{2,1,0:T(8,128)(2,1)S(1)}) custom-call(f32[59,4096]{1,0:T(8,128)S(1)} %copy-done, s32[16,256]{1,0:T(8,128)S(1)} %copy-done.1, f32[16,3,256]{2,1,0:T(4,128)S(1)} %copy.11.grad_ref), custom_call_target="tpu_custom_call" | custom-call | flops 10000000 | bytes 4000000 | tf_op jit(solution)/shard_map/prepare/pallas_call | solution.py:475
  12.4 3.4 %all-to-all-done = s32[16,1,256]{2,1,0:T(1,128)S(1)} async-done(((s32[16,1,256]{2,1,0:T(1,128)}), s32[16,1,256]{2,1,0:T(1,128)S(1)}, u32[]{:S(2)}, u32[]{:S(2)}) %all-to-all-start) | async-done | bytes 16416 | tf_op jit(solution)/shard_map/all_to_all | solution.py:473
  15.9 0.0 copy-start.2
  15.9 0.7 %copy-done.2 = f32[3,8]{1,0:T(4,128)S(1)} copy-done((f32[3,8]{1,0:T(4,128)S(1)}, f32[3,8]{1,0:T(4,128)}, u32[]{:S(2)}) %copy-start.2) | copy-done | bytes 120
  16.5 3.7 %owner.1 = (f32[288,128]{1,0:T(8,128)S(1)}, s32[16,256]{1,0:T(8,128)S(1)}) custom-call(s32[16,256]{1,0:T(8,128)S(1)} %bitcast.10, f32[2,944,128]{2,1,0:T(8,128)S(1)} %get-tuple-element.10.dense_ref, f32[3,8]{1,0:T(4,128)S(1)} %copy-done.2), custom_call_target="tpu_custom_call" | custom-call | flops 10000000 | bytes 4000000 | tf_op jit(solution)/shard_map/owner/pallas_call | solution.py:488
  20.2 10.8 %all_to_all.21 = f32[16,1,2304]{2,1,0:T(1,128)S(1)} all-to-all(f32[16,1,2304]{2,1,0:T(1,128)S(1)} %bitcast.9), channel_id=1, replica_groups=mesh['groups'=2,'gs'=16] {'gs'}, dimensions={0} | all-to-all | bytes 294912 | tf_op jit(solution)/shard_map/all_to_all | solution.py:457
  31.0 0.0 copy-start.3
  31.0 0.0 copy-start.4
  31.0 0.7 %copy-done.3 = s32[16]{0:T(128)S(1)} copy-done((s32[16]{0:T(128)S(1)}, s32[16]{0:T(128)}, u32[]{:S(2)}) %copy-start.3) | copy-done | bytes 88
  31.7 0.0 copy-done.4
  31.7 18.4 %render.1 = (f32[16,3,256]{2,1,0:T(4,128)S(1)}, f32[288,128]{1,0:T(8,128)}) custom-call(f32[288,128]{1,0:T(8,128)S(1)} %bitcast.8, s32[16,256]{1,0:T(8,128)S(1)} %copy-done.1, s32[16,256]{1,0:T(8,128)S(1)} %get-tuple-element.12.inverse_ref, bf16[256,256]{1,0:T(8,128)(2,1)S(1)} %get-tuple-element.13.light_ref, ...), custom_call_target="tpu_custom_call" | custom-call | flops 100000000 | bytes 4000000 | tf_op jit(solution)/shard_map/render/pallas_call | solution.py:497
  50.1 3.5 %all-to-all-start.2 = ((f32[16,1,2304]{2,1,0:T(1,128)}), f32[16,1,2304]{2,1,0:T(1,128)S(1)}, u32[]{:S(2)}, u32[]{:S(2)}) async-start(f32[16,1,2304]{2,1,0:T(1,128)} %bitcast.2), calls=%async_computation.2 | async-start | bytes 294912 | tf_op jit(solution)/shard_map/all_to_all | solution.py:457
  53.6 0.6 copy.14
  54.3 7.5 %all-to-all-done.2 = f32[16,1,2304]{2,1,0:T(1,128)S(1)} async-done(((f32[16,1,2304]{2,1,0:T(1,128)}), f32[16,1,2304]{2,1,0:T(1,128)S(1)}, u32[]{:S(2)}, u32[]{:S(2)}) %all-to-all-start.2) | async-done | bytes 147488 | tf_op jit(solution)/shard_map/all_to_all | solution.py:457
  61.8 3.3 %return.1 = f32[59,4096]{1,0:T(8,128)} custom-call(f32[288,128]{1,0:T(8,128)S(1)} %bitcast.7, s32[16,256]{1,0:T(8,128)S(1)} %get-tuple-element.17.inverse_ref, f32[2,944,128]{2,1,0:T(8,128)S(1)} %get-tuple-element.10.dense_ref, f32[3,8]{1,0:T(4,128)S(1)} %copy-done.2), custom_call_target="tpu_custom_call" | custom-call | flops 10000000 | bytes 4000000 | tf_op jit(solution)/shard_map/return/pallas_call | solution.py:515
  (2 shorter events, 0.0 us)
Async XLA Ops:
  0.6 8.7 %copy-start.5 = (f32[16,3,256]{2,0,1:T(8,128)S(1)}, f32[16,3,256]{2,0,1:T(8,128)}, u32[]{:S(2)}) copy-start(f32[16,3,256]{2,0,1:T(8,128)} %param.13) | copy-start | bytes 147460
  2.0 13.9 %all-to-all-start = ((s32[16,1,256]{2,1,0:T(1,128)}), s32[16,1,256]{2,1,0:T(1,128)S(1)}, u32[]{:S(2)}, u32[]{:S(2)}) async-start(s32[16,1,256]{2,1,0:T(1,128)} %all_to_all.13), calls=%async_computation | async-start | bytes 32768 | tf_op jit(solution)/shard_map/all_to_all | solution.py:473
  9.4 0.7 %copy-start.1 = (s32[16,256]{1,0:T(8,128)S(1)}, s32[16,256]{1,0:T(8,128)}, u32[]{:S(2)}) copy-start(s32[16,256]{1,0:T(8,128)} %member_ref.3) | copy-start | bytes 49156
  10.1 1.2 %copy-start = (f32[59,4096]{1,0:T(8,128)S(1)}, f32[59,4096]{1,0:T(8,128)}, u32[]{:S(2)}) copy-start(f32[59,4096]{1,0:T(8,128)} %params_ref.1) | copy-start | bytes 2899972
  15.9 0.7 %copy-start.2 = (f32[3,8]{1,0:T(4,128)S(1)}, f32[3,8]{1,0:T(4,128)}, u32[]{:S(2)}) copy-start(f32[3,8]{1,0:T(4,128)} %cam_ref.3) | copy-start | bytes 292
  31.0 0.7 %copy-start.3 = (s32[16]{0:T(128)S(1)}, s32[16]{0:T(128)}, u32[]{:S(2)}) copy-start(s32[16]{0:T(128)} %length_ref.1) | copy-start | bytes 196
  31.0 0.7 %copy-start.4 = (s32[16]{0:T(128)S(1)}, s32[16]{0:T(128)}, u32[]{:S(2)}) copy-start(s32[16]{0:T(128)} %place_ref.1) | copy-start | bytes 196
  50.1 11.7 %all-to-all-start.2 = ((f32[16,1,2304]{2,1,0:T(1,128)}), f32[16,1,2304]{2,1,0:T(1,128)S(1)}, u32[]{:S(2)}, u32[]{:S(2)}) async-start(f32[16,1,2304]{2,1,0:T(1,128)} %bitcast.2), calls=%async_computation.2 | async-start | bytes 294912 | tf_op jit(solution)/shard_map/all_to_all | solution.py:457
where the time goes:
time: 65.9 us; the launch traced here: 65.1 us
  Pallas kernels  26.6 us (40%)
  starting transfers between devices  10.9 us (17%)
  waiting for transfers between devices  10.9 us (17%)
  blocking collectives  10.8 us (16%)
  local copies, waits for them, and re-layouts  5.26 us (8%)
  between operations  0.7 us (1%)
    pallas_call x1, Pallas kernels, on_device(): call(functools.partial(render_kernel, packed), 'render', vmem(5) + smem(2...  18.4 us
    all_to_all x1, blocking collectives, travel(): parts = lax.all_to_all(parts, 'gs', split_axis=0, concat_axis=0, tiled=True)  10.8 us
    all_to_all x1, waiting for transfers between devices, travel(): parts = lax.all_to_all(parts, 'gs', split_axis=0, concat_axis=0, tiled=True)  7.53 us
    all_to_all x1, starting transfers between devices, on_device(): lax.all_to_all(requests, 'gs', split_axis=0, concat_axis=0, tiled=True)  7.36 us
    unnamed x15, local copies, waits for them, and re-layouts  3.92 us
    pallas_call x1, Pallas kernels, on_device(): call(functools.partial(owner_kernel, slots, packed), 'owner', vmem(2) + s...  3.69 us
    all_to_all x1, starting transfers between devices, travel(): parts = lax.all_to_all(parts, 'gs', split_axis=0, concat_axis=0, tiled=True)  3.52 us
    all_to_all x1, waiting for transfers between devices, on_device(): lax.all_to_all(requests, 'gs', split_axis=0, concat_axis=0, tiled=True)  3.41 us
  transfers between devices with their start and end apart: 2, of which 2 were waited for; matrix products, arithmetic and copies ran while one was open for 1% of the time, Pallas kernels for 2%

commit v1 on v0

--- a/solution.py
+++ b/solution.py
@@ -15,6 +15,7 @@
 ACROSS = 240
 SCALE = 1920.0
 LOG2E = 1.4426950408889634
+GROUP = 2
 FAR = -1.0e9
 
 sh_c0 = 0.28209479177387814
@@ -191,7 +192,30 @@
                 ]
 
 
-def prepare_kernel(params_ref, member_ref, grad_ref, dense_ref, inverse_ref, light_ref, turned_ref, light):
+def spread_scalars(values, tiles):
+    rows = lax.broadcasted_iota(i32, (tiles, WIDE), 0)
+    out = jnp.full((tiles, WIDE), values[0], values[0].dtype)
+    for t in range(1, tiles):
+        out = jnp.where(rows == t, values[t], out)
+    return out
+
+
+def prepare_kernel(
+    params_ref,
+    member_ref,
+    grad_ref,
+    length_ref,
+    place_ref,
+    cam_ref,
+    dense_ref,
+    inverse_ref,
+    light_ref,
+    turned_ref,
+    centre_ref,
+    camera_ref,
+    plan_ref,
+    light,
+):
     width, count = params_ref.shape
     blocks = count // WIDE
     for first in range(0, width, 8):
@@ -210,16 +234,36 @@
     light_ref[...] = light[...].astype(bf16)
     for t in range(tiles):
         turned_ref[t] = light[16 * t : 16 * t + 16, :].T.astype(bf16)
-
-
-def shifts(inverse, slots_per, cam_ref):
+    across = [lax.rem(place_ref[t], ACROSS).astype(f32) for t in range(tiles)]
+    down = [lax.div(place_ref[t], ACROSS).astype(f32) for t in range(tiles)]
+    centre_ref[0] = spread_scalars([(x * SIDE + SIDE / 2) / SCALE - 1.0 for x in across], tiles)
+    centre_ref[1] = spread_scalars([(y * SIDE + SIDE / 2) / SCALE - 0.5625 for y in down], tiles)
+    lengths = spread_scalars([length_ref[t] for t in range(tiles)], tiles)
+    live = lax.broadcasted_iota(i32, (tiles, WIDE), 1) < lengths
+    centre_ref[2] = jnp.where(live, 1.0, 0.0)
     views = cam_ref.shape[1]
+    for axis in range(3):
+        for k in range(views):
+            row = axis * views + k
+            camera_ref[row : row + 1, :] = jnp.full((1, WIDE), cam_ref[axis, k], f32)
+    wide = [(length_ref[t] > WIDE // 2).astype(i32) for t in range(tiles)]
+    many = sum(wide[1:], wide[0])
+    first, last = jnp.int32(0), many
+    for t in range(tiles):
+        plan_ref[jnp.where(wide[t] > 0, first, last)] = t
+        first, last = first + wide[t], last + 1 - wide[t]
+    plan_ref[tiles] = lax.div(many + GROUP - 1, GROUP)
+
+
+def shifts(inverse, slots_per, camera_ref):
+    views = camera_ref.shape[0] // 3
     view = lax.rem(lax.div(inverse, slots_per), views)
     out = []
     for axis in range(3):
-        value = jnp.full(inverse.shape, cam_ref[axis, 0], f32)
+        rows = [camera_ref[axis * views + k : axis * views + k + 1, :] for k in range(views)]
+        value = jnp.broadcast_to(rows[0], inverse.shape)
         for k in range(1, views):
-            value = jnp.where(view == k, cam_ref[axis, k], value)
+            value = jnp.where(view == k, rows[k], value)
         out.append(value)
     return out
 
@@ -228,11 +272,11 @@
     return [get(ref, k * blocks, blocks) for k in range(count)]
 
 
-def owner_kernel(slots_per, packed, asked_ref, dense_ref, cam_ref, attrs_ref, inverse_ref, held):
+def owner_kernel(slots_per, packed, asked_ref, dense_ref, camera_ref, attrs_ref, inverse_ref, held):
     blocks = asked_ref.shape[0]
     width = dense_ref.shape[1] // blocks
     invert(asked_ref, inverse_ref)
-    shift = shifts(inverse_ref[...], slots_per, cam_ref)
+    shift = shifts(inverse_ref[...], slots_per, camera_ref)
     attrs = project(dense_rows(dense_ref, width, blocks), shift)
     for a in range(8):
         put(held, a, blocks, attrs[a], 8)
@@ -240,7 +284,7 @@
     permute(held, asked_ref, 3, functools.partial(put_travel, attrs_ref, blocks, packed))
 
 
-def return_kernel(slots_per, packed, back_ref, inverse_ref, dense_ref, cam_ref, out_ref, held, flat, grads):
+def return_kernel(slots_per, packed, back_ref, inverse_ref, dense_ref, camera_ref, out_ref, held, flat, grads):
     blocks = inverse_ref.shape[0]
     width = dense_ref.shape[1] // blocks
     take_travel(back_ref, held, blocks, packed)
@@ -250,7 +294,7 @@
         put(flat, 8 * blocks + j, 1, ninth)
 
     permute(held, inverse_ref, 2, give)
-    shift = shifts(inverse_ref[...], slots_per, cam_ref)
+    shift = shifts(inverse_ref[...], slots_per, camera_ref)
     _, back = jax.vjp(lambda rows: project(rows, shift), dense_rows(dense_ref, width, blocks))
     (rows,) = back(dense_rows(flat, ATTRS, blocks))
     for k in range(width):
@@ -262,14 +306,6 @@
             out_ref[first : first + count, WIDE * j : WIDE * (j + 1)] = value
 
 
-def spread_scalars(values, tiles):
-    rows = lax.broadcasted_iota(i32, (tiles, WIDE), 0)
-    out = jnp.full((tiles, WIDE), values[0], values[0].dtype)
-    for t in range(1, tiles):
-        out = jnp.where(rows == t, values[t], out)
-    return out
-
-
 def offsets(index):
     column = lax.rem(index, SIDE).astype(f32) - (SIDE - 1) / 2
     row = lax.div(index, SIDE).astype(f32) - (SIDE - 1) / 2
@@ -290,8 +326,8 @@
     inverse_ref,
     light_ref,
     turned_ref,
-    length_ref,
-    place_ref,
+    centre_ref,
+    plan_ref,
     image_ref,
     back_ref,
     held,
@@ -315,12 +351,8 @@
     permute(held, member_ref, 3, give)
 
     mu, nu, con_a, con_b, con_c, opacity, *colors = dense_rows(flat, ATTRS, blocks)
-    across = [lax.rem(place_ref[t], ACROSS).astype(f32) for t in range(tiles)]
-    down = [lax.div(place_ref[t], ACROSS).astype(f32) for t in range(tiles)]
-    centre_u = spread_scalars([(x * SIDE + SIDE / 2) / SCALE - 1.0 for x in across], tiles)
-    centre_v = spread_scalars([(y * SIDE + SIDE / 2) / SCALE - 0.5625 for y in down], tiles)
-    lengths = spread_scalars([length_ref[t] for t in range(tiles)], tiles)
-    live = lax.broadcasted_iota(i32, (tiles, WIDE), 1) < lengths
+    centre_u, centre_v, live = (centre_ref[k] for k in range(3))
+    live = live > 0.0
     m = (mu - centre_u) * SCALE
     n = (nu - centre_v) * SCALE
     unit = LOG2E / (SCALE * SCALE)
@@ -361,45 +393,46 @@
     ).astype(bf16)
     sums[...] = jnp.zeros_like(sums)
 
-    def one_tile(t, many):
-        block = pl.ds(pl.multiple_of(16 * t, 16), 16)
-        coef = get(coefs, t, 32, tiles, many).astype(bf16)
-        color = get(coefs, t + 32 * tiles, 16, tiles, many).astype(bf16)
-        power = jnp.exp2(dot(monomials[...], coef))
-        alpha = jnp.minimum(power, 0.99)
-        keep = 1.0 - alpha
-        high, low = pieces(jnp.log2(keep), 2)
+    def some_tiles(turn, many):
+        ts = [plan_ref[GROUP * turn + k] for k in range(GROUP)]
+        block = [pl.ds(pl.multiple_of(16 * t, 16), 16) for t in ts]
+        coef = [get(coefs, t, 32, tiles, many).astype(bf16) for t in ts]
+        color = [get(coefs, t + 32 * tiles, 16, tiles, many).astype(bf16) for t in ts]
+        power = [jnp.exp2(dot(monomials[...], x)) for x in coef]
+        alpha = [jnp.minimum(x, 0.99) for x in power]
+        keep = [1.0 - x for x in alpha]
+        parts = [pieces(jnp.log2(x), 2) for x in keep]
         before = upper[:many, :many]
-        through = jnp.exp2(dot(high, before) + dot(low, before))
-        weight = alpha * through
-        high, low = pieces(weight, 2)
-        picture = dot_nt(color, high) + dot_nt(color, low)
-        image_ref[t] = picture[0:3] + picture[6:9]
-        tint = dot(light_ref[block, :], high) + dot(light_ref[block, :], low)
-        pull = dot(turned_ref[t], color)
-        high, low = pieces(pull * weight, 2)
+        through = [jnp.exp2(dot(high, before) + dot(low, before)) for high, low in parts]
+        pull = [dot(turned_ref[t], x) for t, x in zip(ts, color)]
+        weight = [x * y for x, y in zip(alpha, through)]
+        parts = [pieces(x * y, 2) for x, y in zip(pull, weight)]
         after = lower[:many, :many]
-        behind = dot(high, after) + dot(low, after)
-        slope = (pull * through - behind / keep) * alpha
-        high, low = pieces(jnp.where(power < 0.99, slope, 0.0), 2)
-        moment = dot(moments[...], high) + dot(moments[...], low)
-        put(sums, pl.multiple_of(16 * t, 16), 8, moment[0:8])
-        put(sums, pl.multiple_of(16 * t + 8, 8), 8, tint[0:8] + pltpu.roll(tint[0:8], 5, 0))
-
-    def step(t, carry):
-        short = length_ref[t] <= WIDE // 2
-
-        @pl.when(short)
-        def _():
-            one_tile(t, WIDE // 2)
-
-        @pl.when(jnp.logical_not(short))
-        def _():
-            one_tile(t, WIDE)
-
+        behind = [dot(high, after) + dot(low, after) for high, low in parts]
+        parts = [pieces(x, 2) for x in weight]
+        for t, x, (high, low) in zip(ts, color, parts):
+            picture = dot_nt(x, high) + dot_nt(x, low)
+            image_ref[t] = picture[0:3] + picture[6:9]
+        for t, rows, (high, low) in zip(ts, block, parts):
+            tint = dot(light_ref[rows, :], high) + dot(light_ref[rows, :], low)
+            put(sums, pl.multiple_of(16 * t + 8, 8), 8, tint[0:8] + pltpu.roll(tint[0:8], 5, 0))
+        for k, t in enumerate(ts):
+            slope = (pull[k] * through[k] - behind[k] / keep[k]) * alpha[k]
+            high, low = pieces(jnp.where(power[k] < 0.99, slope, 0.0), 2)
+            moment = dot(moments[...], high) + dot(moments[...], low)
+            put(sums, pl.multiple_of(16 * t, 16), 8, moment[0:8])
+
+    def wide_turn(turn, carry):
+        some_tiles(turn, WIDE)
         return carry
 
-    lax.fori_loop(0, tiles, step, 0)
+    def narrow_turn(turn, carry):
+        some_tiles(turn, WIDE // 2)
+        return carry
+
+    wide_turns = plan_ref[tiles]
+    lax.fori_loop(0, wide_turns, wide_turn, 0)
+    lax.fori_loop(wide_turns, tiles // GROUP, narrow_turn, 0)
 
     m_xx, m_xy, m_yy, m_x, m_y, m_one = [get(sums, k, tiles, 16) for k in range(6)]
     d_x = m_x - m * m_one
@@ -435,12 +468,12 @@
     return jax.ShapeDtypeStruct(dims, dtype)
 
 
-def call(kernel, name, ins, outs, scratch, cycles):
+def call(kernel, name, ins, outs, scratch, cycles, scalars=0):
     return pl.pallas_call(
         kernel,
         out_shape=outs,
         in_specs=ins,
-        out_specs=vmem(len(outs)),
+        out_specs=vmem(len(outs) - scalars) + smem(scalars),
         scratch_shapes=scratch,
         name=name,
         compiler_params=pltpu.CompilerParams(vmem_limit_bytes=48 * 1024 * 1024),
@@ -472,32 +505,36 @@
 
     asked = lax.all_to_all(requests, "gs", split_axis=0, concat_axis=0, tiled=True)
     asked = asked.reshape(blocks, WIDE)
-    dense, inverse, light, turned = call(
+    dense, inverse, light, turned, centre, camera, plan = call(
         prepare_kernel,
         "prepare",
-        vmem(3),
+        vmem(3) + smem(3),
         [
             shape(2, width * blocks, 128),
             index,
             shape(16 * tiles, WIDE, dtype=bf16),
             shape(tiles, WIDE, 16, dtype=bf16),
+            shape(3, tiles, WIDE),
+            shape(3 * cam_shift.shape[1], WIDE),
+            shape(tiles + 1, dtype=i32),
         ],
         [pltpu.VMEM((16 * tiles, WIDE), f32)],
         10_000_000,
-    )(params, member, pixel_grad)
+        scalars=1,
+    )(params, member, pixel_grad, tile_len, tile_pos, cam_shift)
     attrs, place = call(
         functools.partial(owner_kernel, slots, packed),
         "owner",
-        vmem(2) + smem(1),
+        vmem(3),
         [rows, index],
         [held],
         10_000_000,
-    )(asked, dense, cam_shift)
+    )(asked, dense, camera)
     arrived = travel(attrs, peers, slots, packed)
     image, back = call(
         functools.partial(render_kernel, packed),
         "render",
-        vmem(5) + smem(2),
+        vmem(6) + smem(1),
         [shape(tiles, 3, WIDE), rows],
         [
             held,
@@ -510,16 +547,16 @@
             pltpu.VMEM((16, WIDE), bf16),
         ],
         100_000_000,
-    )(arrived, member, inverse, light, turned, tile_len, tile_pos)
+    )(arrived, member, inverse, light, turned, centre, plan)
     returned = travel(back, peers, slots, packed)
     (grad_params,) = call(
         functools.partial(return_kernel, slots, packed),
         "return",
-        vmem(3) + smem(1),
+        vmem(4),
         [shape(width, count)],
         [held, held, pltpu.VMEM((2, width * blocks, 128), f32)],
         10_000_000,
-    )(returned, place, dense, cam_shift)
+    )(returned, place, dense, camera)
     return (image, grad_params)
 
 

time: 65.9 us -> 57.2 us (0.87)
  Pallas kernels: 26.6 us -> 19.8 us
  local copies, waits for them, and re-layouts: 5.26 us -> 3.89 us
  waiting for transfers between devices: 10.9 us -> 9.83 us
  blocking collectives: 10.8 us -> 11.7 us
    pallas_call x4, Pallas kernels: 26.6 us -> 19.8 us  [the longest x1 11.7 us: on_device(): call(functools.partial(render_kernel, packed), 'render', vmem(6) + smem(1...]
    unnamed x15, local copies, waits for them, and re-layouts: 3.92 us -> 2.55 us
    all_to_all x1, waiting for transfers between devices: 3.41 us -> 2.3 us  [on_device(): lax.all_to_all(requests, 'gs', split_axis=0, concat_axis=0, tiled=True)]
    all_to_all x1, blocking collectives: 10.8 us -> 11.7 us  [travel(): parts = lax.all_to_all(parts, 'gs', split_axis=0, concat_axis=0, tiled=True)]
  transfers between devices with their start and end apart: 2 -> 2, of which waited for: 2 -> 2; matrix products, arithmetic and copies ran while one was open for 1% -> 1% of each run, Pallas kernels for 2% -> 4%
where the time goes in v1:
time: 57.2 us; the launch traced here: 56.9 us
  Pallas kernels  19.8 us (35%)
  blocking collectives  11.7 us (20%)
  starting transfers between devices  10.9 us (19%)
  waiting for transfers between devices  9.83 us (17%)
  local copies, waits for them, and re-layouts  3.89 us (7%)
  between operations  0.73 us (1%)
    all_to_all x1, blocking collectives, travel(): parts = lax.all_to_all(parts, 'gs', split_axis=0, concat_axis=0, tiled=True)  11.7 us
    pallas_call x1, Pallas kernels, on_device(): call(functools.partial(render_kernel, packed), 'render', vmem(6) + smem(1...  11.7 us
    all_to_all x1, waiting for transfers between devices, travel(): parts = lax.all_to_all(parts, 'gs', split_axis=0, concat_axis=0, tiled=True)  7.53 us
    all_to_all x1, starting transfers between devices, on_device(): lax.all_to_all(requests, 'gs', split_axis=0, concat_axis=0, tiled=True)  7.36 us
    all_to_all x1, starting transfers between devices, travel(): parts = lax.all_to_all(parts, 'gs', split_axis=0, concat_axis=0, tiled=True)  3.52 us
    pallas_call x1, Pallas kernels, on_device(): call(functools.partial(owner_kernel, slots, packed), 'owner', vmem(3), [r...  3.12 us
    pallas_call x1, Pallas kernels, on_device(): call(functools.partial(return_kernel, slots, packed), 'return', vmem(4),...  2.78 us
    unnamed x15, local copies, waits for them, and re-layouts  2.55 us
  transfers between devices with their start and end apart: 2, of which 2 were waited for; matrix products, arithmetic and copies ran while one was open for 1% of the time, Pallas kernels for 4%

profile of v1, /device:TPU:0, one launch (start us, length us, event | category | flops | bytes accessed | tf_op | source)
XLA Modules:
  0.0 56.9 jit_solution(4931835978711054724)
XLA Ops:
  0.6 0.0 copy-start.5
  0.6 1.3 %all_to_all.13 = s32[16,1,256]{2,1,0:T(1,128)} reshape(s32[16,256]{1,0:T(8,128)} %param.8) | data formatting | bytes 32768 | tf_op jit(solution)/shard_map/all_to_all | solution.py:506
  2.0 7.4 %all-to-all-start = ((s32[16,1,256]{2,1,0:T(1,128)}), s32[16,1,256]{2,1,0:T(1,128)S(1)}, u32[]{:S(2)}, u32[]{:S(2)}) async-start(s32[16,1,256]{2,1,0:T(1,128)} %all_to_all.13), calls=%async_computation | async-start | bytes 32768 | tf_op jit(solution)/shard_map/all_to_all | solution.py:506
  9.4 0.0 copy-done.5
  9.4 0.0 copy-start.1
  9.4 0.0 copy-start.2
  9.4 0.0 copy-start.3
  9.4 0.0 copy-start.4
  9.5 0.6 %copy-done.1 = s32[16,256]{1,0:T(8,128)S(1)} copy-done((s32[16,256]{1,0:T(8,128)S(1)}, s32[16,256]{1,0:T(8,128)}, u32[]{:S(2)}) %copy-start.1) | copy-done | bytes 16408
  10.1 0.0 copy-done.2
  10.1 0.0 copy-done.3
  10.1 0.0 copy-done.4
  10.1 0.0 copy-start
  10.1 1.2 %copy-done = f32[59,4096]{1,0:T(8,128)S(1)} copy-done((f32[59,4096]{1,0:T(8,128)S(1)}, f32[59,4096]{1,0:T(8,128)}, u32[]{:S(2)}) %copy-start) | copy-done | bytes 966680
  11.3 2.2 %prepare.1 = (f32[2,944,128]{2,1,0:T(8,128)S(1)}, s32[16,256]{1,0:T(8,128)S(1)}, bf16[256,256]{1,0:T(8,128)(2,1)S(1)}, bf16[16,256,16]{2,1,0:T(8,128)(2,1)S(1)},...) custom-call(f32[59,4096]{1,0:T(8,128)S(1)} %copy-done, s32[16,256]{1,0:T(8,128)S(1)} %copy-done.1, ...), custom_call_target="tpu_custom_call" | custom-call | flops 10000000 | bytes 4000000 | tf_op jit(solution)/shard_map/prepare/pallas_call | solution.py:508
  13.5 2.3 %all-to-all-done = s32[16,1,256]{2,1,0:T(1,128)S(1)} async-done(((s32[16,1,256]{2,1,0:T(1,128)}), s32[16,1,256]{2,1,0:T(1,128)S(1)}, u32[]{:S(2)}, u32[]{:S(2)}) %all-to-all-start) | async-done | bytes 16416 | tf_op jit(solution)/shard_map/all_to_all | solution.py:506
  15.9 3.1 %owner.1 = (f32[288,128]{1,0:T(8,128)S(1)}, s32[16,256]{1,0:T(8,128)S(1)}) custom-call(s32[16,256]{1,0:T(8,128)S(1)} %bitcast.10, f32[2,944,128]{2,1,0:T(8,128)S(1)} %get-tuple-element.13.dense_ref, f32[24,256]{1,0:T(8,128)S(1)} %get-tuple-element.14.camera_ref), custom_call_target="tpu_custom_call" | custom-call | flops 10000000 | bytes 4000000 | tf_op jit(solution)/shard_map/owner/pallas_call | solution.py:525
  19.0 11.7 %all_to_all.21 = f32[16,1,2304]{2,1,0:T(1,128)S(1)} all-to-all(f32[16,1,2304]{2,1,0:T(1,128)S(1)} %bitcast.9), channel_id=1, replica_groups=mesh['groups'=2,'gs'=16] {'gs'}, dimensions={0} | all-to-all | bytes 294912 | tf_op jit(solution)/shard_map/all_to_all | solution.py:490
  30.7 11.7 %render.1 = (f32[16,3,256]{2,1,0:T(4,128)S(1)}, f32[288,128]{1,0:T(8,128)}) custom-call(f32[288,128]{1,0:T(8,128)S(1)} %bitcast.8, s32[16,256]{1,0:T(8,128)S(1)} %copy-done.1, s32[16,256]{1,0:T(8,128)S(1)} %get-tuple-element.16.inverse_ref, bf16[256,256]{1,0:T(8,128)(2,1)S(1)} %get-tuple-element.17.light_ref, ...), custom_call_target="tpu_custom_call" | custom-call | flops 100000000 | bytes 4000000 | tf_op jit(solution)/shard_map/render/pallas_call | solution.py:534
  42.4 3.5 %all-to-all-start.2 = ((f32[16,1,2304]{2,1,0:T(1,128)}), f32[16,1,2304]{2,1,0:T(1,128)S(1)}, u32[]{:S(2)}, u32[]{:S(2)}) async-start(f32[16,1,2304]{2,1,0:T(1,128)} %bitcast.2), calls=%async_computation.2 | async-start | bytes 294912 | tf_op jit(solution)/shard_map/all_to_all | solution.py:490
  45.9 0.6 %copy.14 = f32[16,3,256]{2,0,1:T(8,128)} copy(f32[16,3,256]{2,1,0:T(4,128)S(1)} %get-tuple-element.26) | data formatting | bytes 98304
  46.6 7.5 %all-to-all-done.2 = f32[16,1,2304]{2,1,0:T(1,128)S(1)} async-done(((f32[16,1,2304]{2,1,0:T(1,128)}), f32[16,1,2304]{2,1,0:T(1,128)S(1)}, u32[]{:S(2)}, u32[]{:S(2)}) %all-to-all-start.2) | async-done | bytes 147488 | tf_op jit(solution)/shard_map/all_to_all | solution.py:490
  54.1 2.8 %return.1 = f32[59,4096]{1,0:T(8,128)} custom-call(f32[288,128]{1,0:T(8,128)S(1)} %bitcast.7, s32[16,256]{1,0:T(8,128)S(1)} %get-tuple-element.23.inverse_ref, f32[2,944,128]{2,1,0:T(8,128)S(1)} %get-tuple-element.13.dense_ref, f32[24,256]{1,0:T(8,128)S(1)} %get-tuple-element.14.camera_ref), custom_call_target="tpu_custom_call" | custom-call | flops 10000000 | bytes 4000000 | tf_op jit(solution)/shard_map/return/pallas_call | solution.py:552
  (2 shorter events, 0.0 us)
Async XLA Ops:
  0.6 8.7 %copy-start.5 = (f32[16,3,256]{2,0,1:T(8,128)S(1)}, f32[16,3,256]{2,0,1:T(8,128)}, u32[]{:S(2)}) copy-start(f32[16,3,256]{2,0,1:T(8,128)} %param.13) | copy-start | bytes 147460
  2.0 13.9 %all-to-all-start = ((s32[16,1,256]{2,1,0:T(1,128)}), s32[16,1,256]{2,1,0:T(1,128)S(1)}, u32[]{:S(2)}, u32[]{:S(2)}) async-start(s32[16,1,256]{2,1,0:T(1,128)} %all_to_all.13), calls=%async_computation | async-start | bytes 32768 | tf_op jit(solution)/shard_map/all_to_all | solution.py:506
  9.4 0.7 %copy-start.1 = (s32[16,256]{1,0:T(8,128)S(1)}, s32[16,256]{1,0:T(8,128)}, u32[]{:S(2)}) copy-start(s32[16,256]{1,0:T(8,128)} %member_ref.3) | copy-start | bytes 49156
  9.4 0.7 %copy-start.2 = (f32[3,8]{1,0:T(4,128)S(1)}, f32[3,8]{1,0:T(4,128)}, u32[]{:S(2)}) copy-start(f32[3,8]{1,0:T(4,128)} %cam_ref.1) | copy-start | bytes 292
  9.4 0.7 %copy-start.3 = (s32[16]{0:T(128)S(1)}, s32[16]{0:T(128)}, u32[]{:S(2)}) copy-start(s32[16]{0:T(128)} %length_ref.1) | copy-start | bytes 196
  9.4 0.7 %copy-start.4 = (s32[16]{0:T(128)S(1)}, s32[16]{0:T(128)}, u32[]{:S(2)}) copy-start(s32[16]{0:T(128)} %place_ref.1) | copy-start | bytes 196
  10.1 1.2 %copy-start = (f32[59,4096]{1,0:T(8,128)S(1)}, f32[59,4096]{1,0:T(8,128)}, u32[]{:S(2)}) copy-start(f32[59,4096]{1,0:T(8,128)} %params_ref.1) | copy-start | bytes 2899972
  42.4 11.7 %all-to-all-start.2 = ((f32[16,1,2304]{2,1,0:T(1,128)}), f32[16,1,2304]{2,1,0:T(1,128)S(1)}, u32[]{:S(2)}, u32[]{:S(2)}) async-start(f32[16,1,2304]{2,1,0:T(1,128)} %bitcast.2), calls=%async_computation.2 | async-start | bytes 294912 | tf_op jit(solution)/shard_map/all_to_all | solution.py:490

commit v2 on v1

--- a/solution.py
+++ b/solution.py
@@ -15,7 +15,7 @@
 ACROSS = 240
 SCALE = 1920.0
 LOG2E = 1.4426950408889634
-GROUP = 2
+GROUP = 4
 FAR = -1.0e9
 
 sh_c0 = 0.28209479177387814
@@ -115,13 +115,10 @@
     return jnp.dot(one, other, preferred_element_type=f32)
 
 
-def dot_nt(one, other):
-    return lax.dot_general(one, other, (((1,), (1,)), ((), ())), preferred_element_type=f32)
-
-
 def one_hot(low_row):
-    rows = lax.broadcasted_iota(i32, (WIDE, WIDE), 0)
-    return jnp.where(rows == low_row, 1.0, 0.0).astype(bf16)
+    rows = lax.broadcasted_iota(i32, (WIDE, WIDE), 0).astype(f32).astype(bf16)
+    low = jnp.broadcast_to(low_row.astype(f32).astype(bf16), (WIDE, WIDE))
+    return jnp.where(rows == low, jnp.ones((WIDE, WIDE), bf16), jnp.zeros((WIDE, WIDE), bf16))
 
 
 def get(ref, start, count, stride=1, many=WIDE):
@@ -139,27 +136,34 @@
     blocks = index_ref.shape[0]
     high_rows = lax.broadcasted_iota(i32, (blocks, WIDE), 0)
     lanes = lax.broadcasted_iota(i32, (blocks, WIDE), 1).astype(f32)
-    total = jnp.zeros((2 * blocks, WIDE), f32)
+    wide_lanes = lax.broadcasted_iota(i32, (WIDE, WIDE), 1).astype(f32)
+    lows = (index_ref[...] & (WIDE - 1)).astype(f32).T.astype(bf16)
+    thin = wide_lanes.astype(bf16)
+    ones, zeros = jnp.ones((WIDE, WIDE), bf16), jnp.zeros((WIDE, WIDE), bf16)
+    total = None
     for j in range(blocks):
-        row = index_ref[j : j + 1, :]
-        here = high_rows == lax.shift_right_logical(row, 8)
+        here = high_rows == lax.shift_right_logical(index_ref[j : j + 1, :], 8)
         left = jnp.concatenate([jnp.where(here, float(j), 0.0), jnp.where(here, lanes, 0.0)], axis=0)
-        total = total + dot_nt(left.astype(bf16), one_hot(row & (WIDE - 1)))
+        low = jnp.broadcast_to(lows[:, j : j + 1], (WIDE, WIDE))
+        part = dot(left.astype(bf16), jnp.where(thin == low, ones, zeros))
+        total = part if total is None else total + part
     found = total[:blocks] * float(WIDE) + total[blocks:]
     inverse_ref[...] = found.astype(i32)
 
 
 def permute(held_ref, index_ref, count, give):
     blocks = index_ref.shape[0]
-    parts = pieces(get(held_ref, 0, ATTRS * blocks), count)
+    rows = ATTRS * blocks
+    stack = jnp.concatenate(pieces(get(held_ref, 0, rows), count), axis=0)
     high_rows = lax.broadcasted_iota(i32, (blocks, WIDE), 0)
     for j in range(blocks):
         row = index_ref[j : j + 1, :]
         spread = one_hot(row & (WIDE - 1))
         high = lax.shift_right_logical(row, 8)
-        found = dot(parts[0], spread)
-        for part in parts[1:]:
-            found = found + dot(part, spread)
+        both = dot(stack, spread)
+        found = both[:rows]
+        for k in range(1, count):
+            found = found + both[k * rows : (k + 1) * rows]
         high_eight = jnp.broadcast_to(high, (8, WIDE))
         eight = found[0:8]
         for b in range(1, blocks):
@@ -200,14 +204,22 @@
     return out
 
 
+def dense_kernel(params_ref, dense_ref):
+    width, count = params_ref.shape
+    blocks = count // WIDE
+    for first in range(0, width, 8):
+        rows = min(8, width - first)
+        for j in range(blocks):
+            value = params_ref[first : first + rows, WIDE * j : WIDE * (j + 1)]
+            put(dense_ref, first * blocks + j, rows, value, blocks)
+
+
 def prepare_kernel(
-    params_ref,
     member_ref,
     grad_ref,
     length_ref,
     place_ref,
     cam_ref,
-    dense_ref,
     inverse_ref,
     light_ref,
     turned_ref,
@@ -216,24 +228,7 @@
     plan_ref,
     light,
 ):
-    width, count = params_ref.shape
-    blocks = count // WIDE
-    for first in range(0, width, 8):
-        rows = min(8, width - first)
-        for j in range(blocks):
-            value = params_ref[first : first + rows, WIDE * j : WIDE * (j + 1)]
-            put(dense_ref, first * blocks + j, rows, value, blocks)
-    invert(member_ref, inverse_ref)
-    tiles = grad_ref.shape[0]
-    light[...] = jnp.zeros_like(light)
-    for t in range(tiles):
-        high, low = pieces(grad_ref[t], 2)
-        light[16 * t : 16 * t + 3, :] = high.astype(f32)
-        light[16 * t + 3 : 16 * t + 6, :] = low.astype(f32)
-        light[16 * t + 6 : 16 * t + 9, :] = high.astype(f32)
-    light_ref[...] = light[...].astype(bf16)
-    for t in range(tiles):
-        turned_ref[t] = light[16 * t : 16 * t + 16, :].T.astype(bf16)
+    tiles = grad_ref.shape[1]
     across = [lax.rem(place_ref[t], ACROSS).astype(f32) for t in range(tiles)]
     down = [lax.div(place_ref[t], ACROSS).astype(f32) for t in range(tiles)]
     centre_ref[0] = spread_scalars([(x * SIDE + SIDE / 2) / SCALE - 1.0 for x in across], tiles)
@@ -254,6 +249,18 @@
         first, last = first + wide[t], last + 1 - wide[t]
     plan_ref[tiles] = lax.div(many + GROUP - 1, GROUP)
 
+    invert(member_ref, inverse_ref)
+
+    light[...] = jnp.zeros_like(light)
+    for t in range(tiles):
+        high, low = pieces(jnp.concatenate([grad_ref[k, t : t + 1, :] for k in range(3)], axis=0), 2)
+        light[16 * t : 16 * t + 3, :] = high.astype(f32)
+        light[16 * t + 3 : 16 * t + 6, :] = low.astype(f32)
+        light[16 * t + 6 : 16 * t + 9, :] = high.astype(f32)
+    light_ref[...] = light[...].astype(bf16)
+    for t in range(tiles):
+        turned_ref[t] = light[16 * t : 16 * t + 16, :].T.astype(bf16)
+
 
 def shifts(inverse, slots_per, camera_ref):
     views = camera_ref.shape[0] // 3
@@ -330,6 +337,8 @@
     plan_ref,
     image_ref,
     back_ref,
+    image,
+    sent,
     held,
     flat,
     coefs,
@@ -341,7 +350,6 @@
 ):
     tiles = member_ref.shape[0]
     blocks = tiles
-
     take_travel(arrived_ref, held, blocks, packed)
 
     def give(j, eight, ninth):
@@ -411,8 +419,10 @@
         behind = [dot(high, after) + dot(low, after) for high, low in parts]
         parts = [pieces(x, 2) for x in weight]
         for t, x, (high, low) in zip(ts, color, parts):
-            picture = dot_nt(x, high) + dot_nt(x, low)
-            image_ref[t] = picture[0:3] + picture[6:9]
+            turned = x.astype(f32).T.astype(bf16)
+            picture = (dot(high, turned) + dot(low, turned)).T
+            for channel in range(3):
+                image[channel, pl.ds(t, 1), :] = picture[channel : channel + 1] + picture[channel + 6 : channel + 7]
         for t, rows, (high, low) in zip(ts, block, parts):
             tint = dot(light_ref[rows, :], high) + dot(light_ref[rows, :], low)
             put(sums, pl.multiple_of(16 * t + 8, 8), 8, tint[0:8] + pltpu.roll(tint[0:8], 5, 0))
@@ -433,6 +443,8 @@
     wide_turns = plan_ref[tiles]
     lax.fori_loop(0, wide_turns, wide_turn, 0)
     lax.fori_loop(wide_turns, tiles // GROUP, narrow_turn, 0)
+    send = pltpu.make_async_copy(image, image_ref, sent)
+    send.start()
 
     m_xx, m_xy, m_yy, m_x, m_y, m_one = [get(sums, k, tiles, 16) for k in range(6)]
     d_x = m_x - m * m_one
@@ -454,12 +466,17 @@
         put(held, k, blocks, grads[k], 8)
     put(held, 8 * blocks, blocks, grads[8])
     permute(held, inverse_ref, 2, functools.partial(put_travel, back_ref, blocks, packed))
+    send.wait()
 
 
 def vmem(count):
     return [pl.BlockSpec(memory_space=pltpu.VMEM)] * count
 
 
+def far(count):
+    return [pl.BlockSpec(memory_space=pltpu.HBM)] * count
+
+
 def smem(count):
     return [pl.BlockSpec(memory_space=pltpu.SMEM)] * count
 
@@ -468,12 +485,12 @@
     return jax.ShapeDtypeStruct(dims, dtype)
 
 
-def call(kernel, name, ins, outs, scratch, cycles, scalars=0):
+def call(kernel, name, ins, outs, scratch, cycles, places=None):
     return pl.pallas_call(
         kernel,
         out_shape=outs,
         in_specs=ins,
-        out_specs=vmem(len(outs) - scalars) + smem(scalars),
+        out_specs=places or vmem(len(outs)),
         scratch_shapes=scratch,
         name=name,
         compiler_params=pltpu.CompilerParams(vmem_limit_bytes=48 * 1024 * 1024),
@@ -505,12 +522,12 @@
 
     asked = lax.all_to_all(requests, "gs", split_axis=0, concat_axis=0, tiled=True)
     asked = asked.reshape(blocks, WIDE)
-    dense, inverse, light, turned, centre, camera, plan = call(
+    (dense,) = call(dense_kernel, "dense", vmem(1), [shape(2, width * blocks, 128)], [], 1_000_000)(params)
+    inverse, light, turned, centre, camera, plan = call(
         prepare_kernel,
         "prepare",
-        vmem(3) + smem(3),
+        vmem(2) + smem(3),
         [
-            shape(2, width * blocks, 128),
             index,
             shape(16 * tiles, WIDE, dtype=bf16),
             shape(tiles, WIDE, 16, dtype=bf16),
@@ -518,10 +535,12 @@
             shape(3 * cam_shift.shape[1], WIDE),
             shape(tiles + 1, dtype=i32),
         ],
-        [pltpu.VMEM((16 * tiles, WIDE), f32)],
+        [
+            pltpu.VMEM((16 * tiles, WIDE), f32),
+        ],
         10_000_000,
-        scalars=1,
-    )(params, member, pixel_grad, tile_len, tile_pos, cam_shift)
+        vmem(5) + smem(1),
+    )(member, jnp.swapaxes(pixel_grad, 0, 1), tile_len, tile_pos, cam_shift)
     attrs, place = call(
         functools.partial(owner_kernel, slots, packed),
         "owner",
@@ -535,8 +554,10 @@
         functools.partial(render_kernel, packed),
         "render",
         vmem(6) + smem(1),
-        [shape(tiles, 3, WIDE), rows],
+        [shape(3, tiles, WIDE), rows],
         [
+            pltpu.VMEM((3, tiles, WIDE), f32),
+            pltpu.SemaphoreType.DMA,
             held,
             held,
             pltpu.VMEM((2, 48 * tiles, 128), f32),
@@ -547,6 +568,7 @@
             pltpu.VMEM((16, WIDE), bf16),
         ],
         100_000_000,
+        far(1) + vmem(1),
     )(arrived, member, inverse, light, turned, centre, plan)
     returned = travel(back, peers, slots, packed)
     (grad_params,) = call(
@@ -557,7 +579,7 @@
         [held, held, pltpu.VMEM((2, width * blocks, 128), f32)],
         10_000_000,
     )(returned, place, dense, camera)
-    return (image, grad_params)
+    return (jnp.swapaxes(image, 0, 1), grad_params)
 
 
 def solution(mesh):

time: 57.2 us -> 52.8 us (0.923)
  blocking collectives: 11.7 us -> 22.5 us
  waiting for transfers between devices: 9.83 us -> 2.34 us
  Pallas kernels: 19.8 us -> 16.2 us
  starting transfers between devices: 10.9 us -> 7.36 us
  local copies, waits for them, and re-layouts: 3.89 us -> 3.22 us
    all_to_all x1 -> x2, blocking collectives: 11.7 us -> 22.5 us  [travel(): parts = lax.all_to_all(parts, 'gs', split_axis=0, concat_axis=0, tiled=True)]
    all_to_all x1 -> x0, waiting for transfers between devices: 7.53 us -> none  [travel(): parts = lax.all_to_all(parts, 'gs', split_axis=0, concat_axis=0, tiled=True)]
    all_to_all x1 -> x0, starting transfers between devices: 3.52 us -> none  [travel(): parts = lax.all_to_all(parts, 'gs', split_axis=0, concat_axis=0, tiled=True)]
    pallas_call x1, Pallas kernels: 11.7 us -> 9.15 us  [on_device(): call(functools.partial(render_kernel, packed), 'render', vmem(6) + smem(1...]
    pallas_call x1, Pallas kernels: 3.12 us -> 2.38 us  [on_device(): call(functools.partial(owner_kernel, slots, packed), 'owner', vmem(3), [r...]
    unnamed x15 -> x13, local copies, waits for them, and re-layouts: 2.55 us -> 1.89 us
    pallas_call x1 -> x2, Pallas kernels: 2.22 us -> 2.22 us  [the longest x1 1.93 us: on_device(): call(prepare_kernel, 'prepare', vmem(2) + smem(3), [index, shape(16 * til...]
  transfers between devices with their start and end apart: 2 -> 1, of which waited for: 2 -> 1; matrix products, arithmetic and copies ran while one was open for 1% -> 0% of each run, Pallas kernels for 4% -> 4%
where the time goes in v2:
time: 52.8 us; the launch traced here: 52.3 us
  blocking collectives  22.5 us (43%)
  Pallas kernels  16.2 us (31%)
  starting transfers between devices  7.36 us (14%)
  local copies, waits for them, and re-layouts  3.22 us (6%)
  waiting for transfers between devices  2.34 us (4%)
  between operations  0.7 us (1%)
    all_to_all x2, blocking collectives, travel(): parts = lax.all_to_all(parts, 'gs', split_axis=0, concat_axis=0, tiled=True)  22.5 us
    pallas_call x1, Pallas kernels, on_device(): call(functools.partial(render_kernel, packed), 'render', vmem(6) + smem(1...  9.15 us
    all_to_all x1, starting transfers between devices, on_device(): lax.all_to_all(requests, 'gs', split_axis=0, concat_axis=0, tiled=True)  7.36 us
    pallas_call x1, Pallas kernels, on_device(): call(functools.partial(return_kernel, slots, packed), 'return', vmem(4),...  2.41 us
    pallas_call x1, Pallas kernels, on_device(): call(functools.partial(owner_kernel, slots, packed), 'owner', vmem(3), [r...  2.38 us
    all_to_all x1, waiting for transfers between devices, on_device(): lax.all_to_all(requests, 'gs', split_axis=0, concat_axis=0, tiled=True)  2.34 us
    pallas_call x1, Pallas kernels, on_device(): call(prepare_kernel, 'prepare', vmem(2) + smem(3), [index, shape(16 * til...  1.93 us
    unnamed x13, local copies, waits for them, and re-layouts  1.89 us
  transfers between devices with their start and end apart: 1, of which 1 were waited for; matrix products, arithmetic and copies ran while one was open for 0% of the time, Pallas kernels for 4%

profile of v2, /device:TPU:0, one launch (start us, length us, event | category | flops | bytes accessed | tf_op | source)
XLA Modules:
  0.0 52.3 jit_solution(4772745302501366562)
XLA Ops:
  0.6 1.3 %all_to_all.13 = s32[16,1,256]{2,1,0:T(1,128)} reshape(s32[16,256]{1,0:T(8,128)} %param.8) | data formatting | bytes 32768 | tf_op jit(solution)/shard_map/all_to_all | solution.py:523
  2.0 7.4 %all-to-all-start = ((s32[16,1,256]{2,1,0:T(1,128)}), s32[16,1,256]{2,1,0:T(1,128)S(1)}, u32[]{:S(2)}, u32[]{:S(2)}) async-start(s32[16,1,256]{2,1,0:T(1,128)} %all_to_all.13), calls=%async_computation | async-start | bytes 32768 | tf_op jit(solution)/shard_map/all_to_all | solution.py:523
  9.3 0.0 copy-start
  9.3 1.2 %copy-done = f32[59,4096]{1,0:T(8,128)S(1)} copy-done((f32[59,4096]{1,0:T(8,128)S(1)}, f32[59,4096]{1,0:T(8,128)}, u32[]{:S(2)}) %copy-start) | copy-done | bytes 966680
  10.6 0.0 copy-start.1
  10.6 0.0 copy-start.2
  10.6 0.0 copy-start.3
  10.6 0.3 dense.1.dense_ref
  10.9 0.0 copy-start.4
  10.9 0.0 copy-start.5
  10.9 0.4 copy-done.1
  11.3 0.1 copy-done.2
  11.4 0.0 copy-done.3
  11.4 0.2 copy-done.4
  11.5 0.0 copy-done.5
  11.5 1.9 %prepare.1 = (s32[16,256]{1,0:T(8,128)S(1)}, bf16[256,256]{1,0:T(8,128)(2,1)S(1)}, bf16[16,256,16]{2,1,0:T(8,128)(2,1)S(1)}, f32[3,16,256]{2,1,0:T(8,128)S(1)}, f32[24,256]{1,0:T(8,128)S(1)}, /*index=5*/s32[17]{0:T(128)S(1)}) custom-call(s32[16,256]{1,0:T(8,128)S(1)} %copy-done.1, f32[3,16,256]{2,1,0:T(8,128)S(1)} %bitcast.14, s32[16]{0:T(128)S(1)} %copy-done.4, ...), custom_call_target="tpu_custom_call" | custom-call | flops 10000000 | bytes 4000000 | tf_op jit(solution)/shard_map/prepare/pallas_call | solution.py:526
  13.5 2.3 %all-to-all-done = s32[16,1,256]{2,1,0:T(1,128)S(1)} async-done(((s32[16,1,256]{2,1,0:T(1,128)}), s32[16,1,256]{2,1,0:T(1,128)S(1)}, u32[]{:S(2)}, u32[]{:S(2)}) %all-to-all-start) | async-done | bytes 16416 | tf_op jit(solution)/shard_map/all_to_all | solution.py:523
  15.8 2.4 %owner.1 = (f32[288,128]{1,0:T(8,128)S(1)}, s32[16,256]{1,0:T(8,128)S(1)}) custom-call(s32[16,256]{1,0:T(8,128)S(1)} %bitcast.13, f32[2,944,128]{2,1,0:T(8,128)S(1)} %dense.1.dense_ref, f32[24,256]{1,0:T(8,128)S(1)} %get-tuple-element.12.camera_ref), custom_call_target="tpu_custom_call" | custom-call | flops 10000000 | bytes 4000000 | tf_op jit(solution)/shard_map/owner/pallas_call | solution.py:544
  18.2 11.7 %all_to_all.21 = f32[16,1,2304]{2,1,0:T(1,128)S(1)} all-to-all(f32[16,1,2304]{2,1,0:T(1,128)S(1)} %bitcast.12), channel_id=1, replica_groups=mesh['groups'=2,'gs'=16] {'gs'}, dimensions={0} | all-to-all | bytes 294912 | tf_op jit(solution)/shard_map/all_to_all | solution.py:507
  29.9 9.2 %render.1 = (f32[3,16,256]{2,1,0:T(8,128)}, f32[288,128]{1,0:T(8,128)S(1)}) custom-call(f32[288,128]{1,0:T(8,128)S(1)} %bitcast.9, s32[16,256]{1,0:T(8,128)S(1)} %copy-done.1, s32[16,256]{1,0:T(8,128)S(1)} %get-tuple-element.14.inverse_ref, bf16[256,256]{1,0:T(8,128)(2,1)S(1)} %get-tuple-element.15.light_ref, ...), custom_call_target="tpu_custom_call" | custom-call | flops 100000000 | bytes 4000000 | tf_op jit(solution)/shard_map/render/pallas_call | solution.py:553
  39.1 10.8 %all_to_all.22 = f32[16,1,2304]{2,1,0:T(1,128)S(1)} all-to-all(f32[16,1,2304]{2,1,0:T(1,128)S(1)} %bitcast.11), channel_id=1, replica_groups=mesh['groups'=2,'gs'=16] {'gs'}, dimensions={0} | all-to-all | bytes 294912 | tf_op jit(solution)/shard_map/all_to_all | solution.py:507
  49.9 2.4 %return.1 = f32[59,4096]{1,0:T(8,128)} custom-call(f32[288,128]{1,0:T(8,128)S(1)} %bitcast.10, s32[16,256]{1,0:T(8,128)S(1)} %get-tuple-element.21.inverse_ref, f32[2,944,128]{2,1,0:T(8,128)S(1)} %dense.1.dense_ref, f32[24,256]{1,0:T(8,128)S(1)} %get-tuple-element.12.camera_ref), custom_call_target="tpu_custom_call" | custom-call | flops 10000000 | bytes 4000000 | tf_op jit(solution)/shard_map/return/pallas_call | solution.py:574
  (1 shorter events, 0.0 us)
Async XLA Ops:
  2.0 13.9 %all-to-all-start = ((s32[16,1,256]{2,1,0:T(1,128)}), s32[16,1,256]{2,1,0:T(1,128)S(1)}, u32[]{:S(2)}, u32[]{:S(2)}) async-start(s32[16,1,256]{2,1,0:T(1,128)} %all_to_all.13), calls=%async_computation | async-start | bytes 32768 | tf_op jit(solution)/shard_map/all_to_all | solution.py:523
  9.3 1.2 %copy-start = (f32[59,4096]{1,0:T(8,128)S(1)}, f32[59,4096]{1,0:T(8,128)}, u32[]{:S(2)}) copy-start(f32[59,4096]{1,0:T(8,128)} %params_ref.1) | copy-start | bytes 2899972
  10.6 0.7 %copy-start.1 = (s32[16,256]{1,0:T(8,128)S(1)}, s32[16,256]{1,0:T(8,128)}, u32[]{:S(2)}) copy-start(s32[16,256]{1,0:T(8,128)} %member_ref.3) | copy-start | bytes 49156
  10.6 0.8 %copy-start.2 = (f32[16,3,256]{2,0,1:T(8,128)S(1)}, f32[16,3,256]{2,0,1:T(8,128)}, u32[]{:S(2)}) copy-start(f32[16,3,256]{2,0,1:T(8,128)} %param.13) | copy-start | bytes 147460
  10.6 0.8 %copy-start.3 = (f32[3,8]{1,0:T(4,128)S(1)}, f32[3,8]{1,0:T(4,128)}, u32[]{:S(2)}) copy-start(f32[3,8]{1,0:T(4,128)} %cam_ref.1) | copy-start | bytes 292
  10.9 0.7 %copy-start.4 = (s32[16]{0:T(128)S(1)}, s32[16]{0:T(128)}, u32[]{:S(2)}) copy-start(s32[16]{0:T(128)} %length_ref.1) | copy-start | bytes 196
  10.9 0.7 %copy-start.5 = (s32[16]{0:T(128)S(1)}, s32[16]{0:T(128)}, u32[]{:S(2)}) copy-start(s32[16]{0:T(128)} %place_ref.1) | copy-start | bytes 196

commit v3 on v2

--- a/solution.py
+++ b/solution.py
@@ -38,7 +38,7 @@
 )
 
 
-def project(table, shift):
+def outline(table, shift):
     xpos = table[0] - shift[0]
     ypos = table[1] - shift[1]
     zpos = table[2] - shift[2]
@@ -61,6 +61,14 @@
     cov_b = first[0] * second[0] + first[1] * second[1] + first[2] * second[2]
     cov_c = second[0] * second[0] + second[1] * second[1] + second[2] * second[2] + 8e-08
     over_det = 1.0 / (cov_a * cov_c - cov_b * cov_b)
+    opacity = 1.0 / (1.0 + jnp.exp(-table[10]))
+    return [mean_u, mean_v, cov_c * over_det, -cov_b * over_det, cov_a * over_det, opacity]
+
+
+def tints(place, coefs, shift):
+    xpos = place[0] - shift[0]
+    ypos = place[1] - shift[1]
+    zpos = place[2] - shift[2]
     over_length = 1.0 / jnp.sqrt(xpos * xpos + ypos * ypos + zpos * zpos)
     dx, dy, dz = (xpos * over_length, ypos * over_length, zpos * over_length)
     xx, yy, zz = (dx * dx, dy * dy, dz * dz)
@@ -83,22 +91,11 @@
     ]
     colors = []
     for k in range(3):
-        total = 0.5 + sh_c0 * table[11 + 16 * k]
+        total = 0.5 + sh_c0 * coefs[16 * k]
         for j, part in enumerate(basis):
-            total = total + part * table[12 + 16 * k + j]
+            total = total + part * coefs[16 * k + 1 + j]
         colors.append(jnp.maximum(total, 0.0))
-    opacity = 1.0 / (1.0 + jnp.exp(-table[10]))
-    return [
-        mean_u,
-        mean_v,
-        cov_c * over_det,
-        -cov_b * over_det,
-        cov_a * over_det,
-        opacity,
-        colors[0],
-        colors[1],
-        colors[2],
-    ]
+    return colors
 
 
 def pieces(value, count):
@@ -113,6 +110,12 @@
 
 def dot(one, other):
     return jnp.dot(one, other, preferred_element_type=f32)
+
+
+def stacked(high, low, weights):
+    rows = high.shape[0]
+    both = dot(jnp.concatenate([high, low], axis=0), weights)
+    return both[:rows] + both[rows:]
 
 
 def one_hot(low_row):
@@ -151,25 +154,31 @@
     inverse_ref[...] = found.astype(i32)
 
 
-def permute(held_ref, index_ref, count, give):
+def permute(held_ref, index_ref, fine, give):
     blocks = index_ref.shape[0]
     rows = ATTRS * blocks
-    stack = jnp.concatenate(pieces(get(held_ref, 0, rows), count), axis=0)
+    thirds = [pieces(get(held_ref, a, blocks, 8), 3)[2] for a in range(fine)]
+    stack = jnp.concatenate(pieces(get(held_ref, 0, rows), 2) + thirds, axis=0)
     high_rows = lax.broadcasted_iota(i32, (blocks, WIDE), 0)
+    place = lax.broadcasted_iota(i32, (8, WIDE), 0)
     for j in range(blocks):
         row = index_ref[j : j + 1, :]
-        spread = one_hot(row & (WIDE - 1))
         high = lax.shift_right_logical(row, 8)
-        both = dot(stack, spread)
-        found = both[:rows]
-        for k in range(1, count):
-            found = found + both[k * rows : (k + 1) * rows]
+        here = high_rows == high
+        both = dot(stack, one_hot(row & (WIDE - 1)))
+        found = both[:rows] + both[rows : 2 * rows]
         high_eight = jnp.broadcast_to(high, (8, WIDE))
         eight = found[0:8]
         for b in range(1, blocks):
             eight = jnp.where(high_eight == b, found[8 * b : 8 * b + 8], eight)
-        ninth = jnp.sum(jnp.where(high_rows == high, found[8 * blocks :], 0.0), axis=0, keepdims=True)
-        give(j, eight, ninth)
+
+        def single(values):
+            return jnp.sum(jnp.where(here, values, 0.0), axis=0, keepdims=True)
+
+        for a in range(fine):
+            start = 2 * rows + a * blocks
+            eight = eight + jnp.where(place == a, single(both[start : start + blocks]), 0.0)
+        give(j, eight, single(found[8 * blocks :]))
 
 
 def put_travel(out_ref, blocks, packed, j, eight, ninth):
@@ -284,33 +293,57 @@
     width = dense_ref.shape[1] // blocks
     invert(asked_ref, inverse_ref)
     shift = shifts(inverse_ref[...], slots_per, camera_ref)
-    attrs = project(dense_rows(dense_ref, width, blocks), shift)
+    table = dense_rows(dense_ref, width, blocks)
+    attrs = outline(table, shift) + tints(table[:3], table[11:], shift)
     for a in range(8):
         put(held, a, blocks, attrs[a], 8)
     put(held, 8 * blocks, blocks, attrs[8])
-    permute(held, asked_ref, 3, functools.partial(put_travel, attrs_ref, blocks, packed))
-
-
-def return_kernel(slots_per, packed, back_ref, inverse_ref, dense_ref, camera_ref, out_ref, held, flat, grads):
+    permute(held, asked_ref, 2, functools.partial(put_travel, attrs_ref, blocks, packed))
+
+
+def return_kernel(slots_per, packed, back_ref, inverse_ref, dense_ref, camera_ref, out_far, held, flat, grads, out_ref, sent):
     blocks = inverse_ref.shape[0]
     width = dense_ref.shape[1] // blocks
+    half = blocks // 2
     take_travel(back_ref, held, blocks, packed)
+
+    sends = []
+
+    def send_rows(first, near):
+        count = min(8, width - first)
+        for j in range(near, near + half):
+            value = get(grads, first * blocks + j, count, blocks)
+            out_ref[first : first + count, WIDE * j : WIDE * (j + 1)] = value
+        part = (pl.ds(first, count), pl.ds(WIDE * near, WIDE * half))
+        sends.append(pltpu.make_async_copy(out_ref.at[part], out_far.at[part], sent.at[len(sends)]))
+        sends[-1].start()
+
+    def finish(near):
+        table = [get(dense_ref, k * blocks + near, half) for k in range(width)]
+        given = [get(flat, k * blocks + near, half) for k in range(ATTRS)]
+        shift = shifts(inverse_ref[near : near + half, :], slots_per, camera_ref)
+        _, back = jax.vjp(lambda place, coefs: tints(place, coefs, shift), table[:3], table[11:])
+        drift, slopes = back(given[6:])
+        for k in range(11, width):
+            put(grads, k * blocks + near, half, slopes[k - 11])
+        for first in range(16, width, 8):
+            send_rows(first, near)
+        _, back = jax.vjp(lambda rows: outline(rows, shift), table[:11])
+        (slopes,) = back(given[:6])
+        for k in range(11):
+            put(grads, k * blocks + near, half, slopes[k] + drift[k] if k < 3 else slopes[k])
+        for first in range(0, 16, 8):
+            send_rows(first, near)
 
     def give(j, eight, ninth):
         put(flat, j, 8, eight, blocks)
         put(flat, 8 * blocks + j, 1, ninth)
-
-    permute(held, inverse_ref, 2, give)
-    shift = shifts(inverse_ref[...], slots_per, camera_ref)
-    _, back = jax.vjp(lambda rows: project(rows, shift), dense_rows(dense_ref, width, blocks))
-    (rows,) = back(dense_rows(flat, ATTRS, blocks))
-    for k in range(width):
-        put(grads, k * blocks, blocks, rows[k])
-    for first in range(0, width, 8):
-        count = min(8, width - first)
-        for j in range(blocks):
-            value = get(grads, first * blocks + j, count, blocks)
-            out_ref[first : first + count, WIDE * j : WIDE * (j + 1)] = value
+        if (j + 1) % half == 0:
+            finish(j + 1 - half)
+
+    permute(held, inverse_ref, 0, give)
+    for send in sends:
+        send.wait()
 
 
 def offsets(index):
@@ -356,7 +389,7 @@
         put(flat, j, 8, eight, blocks)
         put(flat, 8 * blocks + j, 1, ninth)
 
-    permute(held, member_ref, 3, give)
+    permute(held, member_ref, 2, give)
 
     mu, nu, con_a, con_b, con_c, opacity, *colors = dense_rows(flat, ATTRS, blocks)
     centre_u, centre_v, live = (centre_ref[k] for k in range(3))
@@ -406,30 +439,29 @@
         block = [pl.ds(pl.multiple_of(16 * t, 16), 16) for t in ts]
         coef = [get(coefs, t, 32, tiles, many).astype(bf16) for t in ts]
         color = [get(coefs, t + 32 * tiles, 16, tiles, many).astype(bf16) for t in ts]
-        power = [jnp.exp2(dot(monomials[...], x)) for x in coef]
-        alpha = [jnp.minimum(x, 0.99) for x in power]
-        keep = [1.0 - x for x in alpha]
-        parts = [pieces(jnp.log2(x), 2) for x in keep]
+        alpha = [jnp.minimum(jnp.exp2(dot(monomials[...], x)), 0.99) for x in coef]
+        parts = [pieces(jnp.log2(1.0 - x), 2) for x in alpha]
         before = upper[:many, :many]
-        through = [jnp.exp2(dot(high, before) + dot(low, before)) for high, low in parts]
-        pull = [dot(turned_ref[t], x) for t, x in zip(ts, color)]
+        through = [jnp.exp2(stacked(high, low, before)) for high, low in parts]
         weight = [x * y for x, y in zip(alpha, through)]
-        parts = [pieces(x * y, 2) for x, y in zip(pull, weight)]
-        after = lower[:many, :many]
-        behind = [dot(high, after) + dot(low, after) for high, low in parts]
         parts = [pieces(x, 2) for x in weight]
         for t, x, (high, low) in zip(ts, color, parts):
             turned = x.astype(f32).T.astype(bf16)
-            picture = (dot(high, turned) + dot(low, turned)).T
+            picture = stacked(high, low, turned).T
             for channel in range(3):
                 image[channel, pl.ds(t, 1), :] = picture[channel : channel + 1] + picture[channel + 6 : channel + 7]
-        for t, rows, (high, low) in zip(ts, block, parts):
-            tint = dot(light_ref[rows, :], high) + dot(light_ref[rows, :], low)
+            rows = pl.ds(pl.multiple_of(16 * t, 16), 16)
+            lit = light_ref[rows, :]
+            tint = dot(jnp.concatenate([lit, lit], axis=1), jnp.concatenate([high, low], axis=0))
             put(sums, pl.multiple_of(16 * t + 8, 8), 8, tint[0:8] + pltpu.roll(tint[0:8], 5, 0))
+        pulled = [dot(turned_ref[t], x) * y for t, x, y in zip(ts, color, weight)]
+        parts = [pieces(x, 2) for x in pulled]
+        after = lower[:many, :many]
+        behind = [stacked(high, low, after) for high, low in parts]
         for k, t in enumerate(ts):
-            slope = (pull[k] * through[k] - behind[k] / keep[k]) * alpha[k]
-            high, low = pieces(jnp.where(power[k] < 0.99, slope, 0.0), 2)
-            moment = dot(moments[...], high) + dot(moments[...], low)
+            slope = pulled[k] - behind[k] * (alpha[k] / (1.0 - alpha[k]))
+            high, low = pieces(jnp.where(alpha[k] < 0.99, slope, 0.0), 2)
+            moment = dot(jnp.concatenate([moments[...]] * 2, axis=1), jnp.concatenate([high, low], axis=0))
             put(sums, pl.multiple_of(16 * t, 16), 8, moment[0:8])
 
     def wide_turn(turn, carry):
@@ -465,7 +497,7 @@
     for k in range(8):
         put(held, k, blocks, grads[k], 8)
     put(held, 8 * blocks, blocks, grads[8])
-    permute(held, inverse_ref, 2, functools.partial(put_travel, back_ref, blocks, packed))
+    permute(held, inverse_ref, 0, functools.partial(put_travel, back_ref, blocks, packed))
     send.wait()
 
 
@@ -576,8 +608,15 @@
         "return",
         vmem(4),
         [shape(width, count)],
-        [held, held, pltpu.VMEM((2, width * blocks, 128), f32)],
+        [
+            held,
+            held,
+            pltpu.VMEM((2, width * blocks, 128), f32),
+            pltpu.VMEM((width, count), f32),
+            pltpu.SemaphoreType.DMA((2 * -(-width // 8),)),
+        ],
         10_000_000,
+        far(1),
     )(returned, place, dense, camera)
     return (jnp.swapaxes(image, 0, 1), grad_params)
 

time: 52.8 us -> 51.8 us (0.981)
  Pallas kernels: 16.2 us -> 14.9 us
    pallas_call x1, Pallas kernels: 9.15 us -> 8.25 us  [on_device(): call(functools.partial(render_kernel, packed), 'render', vmem(6) + smem(1...]
where the time goes in v3:
time: 51.8 us; the launch traced here: 51.4 us
  blocking collectives  22.8 us (44%)
  Pallas kernels  14.9 us (29%)
  starting transfers between devices  7.36 us (14%)
  local copies, waits for them, and re-layouts  3.22 us (6%)
  waiting for transfers between devices  2.34 us (5%)
  between operations  0.7 us (1%)
    all_to_all x2, blocking collectives, travel(): parts = lax.all_to_all(parts, 'gs', split_axis=0, concat_axis=0, tiled=True)  22.8 us
    pallas_call x1, Pallas kernels, on_device(): call(functools.partial(render_kernel, packed), 'render', vmem(6) + smem(1...  8.25 us
    all_to_all x1, starting transfers between devices, on_device(): lax.all_to_all(requests, 'gs', split_axis=0, concat_axis=0, tiled=True)  7.36 us
    all_to_all x1, waiting for transfers between devices, on_device(): lax.all_to_all(requests, 'gs', split_axis=0, concat_axis=0, tiled=True)  2.34 us
    pallas_call x1, Pallas kernels, on_device(): call(functools.partial(return_kernel, slots, packed), 'return', vmem(4),...  2.32 us
    pallas_call x1, Pallas kernels, on_device(): call(functools.partial(owner_kernel, slots, packed), 'owner', vmem(3), [r...  2.13 us
    pallas_call x1, Pallas kernels, on_device(): call(prepare_kernel, 'prepare', vmem(2) + smem(3), [index, shape(16 * til...  1.93 us
    unnamed x13, local copies, waits for them, and re-layouts  1.89 us
  transfers between devices with their start and end apart: 1, of which 1 were waited for; matrix products, arithmetic and copies ran while one was open for 0% of the time, Pallas kernels for 4%

profile of v3, /device:TPU:0, one launch (start us, length us, event | category | flops | bytes accessed | tf_op | source)
XLA Modules:
  0.0 51.4 jit_solution(11664807837150492717)
XLA Ops:
  0.6 1.3 %all_to_all.13 = s32[16,1,256]{2,1,0:T(1,128)} reshape(s32[16,256]{1,0:T(8,128)} %param.8) | data formatting | bytes 32768 | tf_op jit(solution)/shard_map/all_to_all | solution.py:555
  2.0 7.4 %all-to-all-start = ((s32[16,1,256]{2,1,0:T(1,128)}), s32[16,1,256]{2,1,0:T(1,128)S(1)}, u32[]{:S(2)}, u32[]{:S(2)}) async-start(s32[16,1,256]{2,1,0:T(1,128)} %all_to_all.13), calls=%async_computation | async-start | bytes 32768 | tf_op jit(solution)/shard_map/all_to_all | solution.py:555
  9.3 0.0 copy-start
  9.3 1.2 %copy-done = f32[59,4096]{1,0:T(8,128)S(1)} copy-done((f32[59,4096]{1,0:T(8,128)S(1)}, f32[59,4096]{1,0:T(8,128)}, u32[]{:S(2)}) %copy-start) | copy-done | bytes 966680
  10.6 0.0 copy-start.1
  10.6 0.0 copy-start.2
  10.6 0.0 copy-start.3
  10.6 0.3 dense.1.dense_ref
  10.9 0.0 copy-start.4
  10.9 0.0 copy-start.5
  10.9 0.4 copy-done.1
  11.3 0.1 copy-done.2
  11.4 0.0 copy-done.3
  11.4 0.2 copy-done.4
  11.5 0.0 copy-done.5
  11.5 1.9 %prepare.1 = (s32[16,256]{1,0:T(8,128)S(1)}, bf16[256,256]{1,0:T(8,128)(2,1)S(1)}, bf16[16,256,16]{2,1,0:T(8,128)(2,1)S(1)}, f32[3,16,256]{2,1,0:T(8,128)S(1)}, f32[24,256]{1,0:T(8,128)S(1)}, /*index=5*/s32[17]{0:T(128)S(1)}) custom-call(s32[16,256]{1,0:T(8,128)S(1)} %copy-done.1, f32[3,16,256]{2,1,0:T(8,128)S(1)} %bitcast.14, s32[16]{0:T(128)S(1)} %copy-done.4, ...), custom_call_target="tpu_custom_call" | custom-call | flops 10000000 | bytes 4000000 | tf_op jit(solution)/shard_map/prepare/pallas_call | solution.py:558
  13.5 2.3 %all-to-all-done = s32[16,1,256]{2,1,0:T(1,128)S(1)} async-done(((s32[16,1,256]{2,1,0:T(1,128)}), s32[16,1,256]{2,1,0:T(1,128)S(1)}, u32[]{:S(2)}, u32[]{:S(2)}) %all-to-all-start) | async-done | bytes 16416 | tf_op jit(solution)/shard_map/all_to_all | solution.py:555
  15.8 2.1 %owner.1 = (f32[288,128]{1,0:T(8,128)S(1)}, s32[16,256]{1,0:T(8,128)S(1)}) custom-call(s32[16,256]{1,0:T(8,128)S(1)} %bitcast.13, f32[2,944,128]{2,1,0:T(8,128)S(1)} %dense.1.dense_ref, f32[24,256]{1,0:T(8,128)S(1)} %get-tuple-element.12.camera_ref), custom_call_target="tpu_custom_call" | custom-call | flops 10000000 | bytes 4000000 | tf_op jit(solution)/shard_map/owner/pallas_call | solution.py:576
  18.0 11.7 %all_to_all.21 = f32[16,1,2304]{2,1,0:T(1,128)S(1)} all-to-all(f32[16,1,2304]{2,1,0:T(1,128)S(1)} %bitcast.12), channel_id=1, replica_groups=mesh['groups'=2,'gs'=16] {'gs'}, dimensions={0} | all-to-all | bytes 294912 | tf_op jit(solution)/shard_map/all_to_all | solution.py:539
  29.6 8.3 %render.1 = (f32[3,16,256]{2,1,0:T(8,128)}, f32[288,128]{1,0:T(8,128)S(1)}) custom-call(f32[288,128]{1,0:T(8,128)S(1)} %bitcast.9, s32[16,256]{1,0:T(8,128)S(1)} %copy-done.1, s32[16,256]{1,0:T(8,128)S(1)} %get-tuple-element.14.inverse_ref, bf16[256,256]{1,0:T(8,128)(2,1)S(1)} %get-tuple-element.15.light_ref, ...), custom_call_target="tpu_custom_call" | custom-call | flops 100000000 | bytes 4000000 | tf_op jit(solution)/shard_map/render/pallas_call | solution.py:585
  37.9 11.1 %all_to_all.22 = f32[16,1,2304]{2,1,0:T(1,128)S(1)} all-to-all(f32[16,1,2304]{2,1,0:T(1,128)S(1)} %bitcast.11), channel_id=1, replica_groups=mesh['groups'=2,'gs'=16] {'gs'}, dimensions={0} | all-to-all | bytes 294912 | tf_op jit(solution)/shard_map/all_to_all | solution.py:539
  49.1 2.3 %return.1 = f32[59,4096]{1,0:T(8,128)} custom-call(f32[288,128]{1,0:T(8,128)S(1)} %bitcast.10, s32[16,256]{1,0:T(8,128)S(1)} %get-tuple-element.21.inverse_ref, f32[2,944,128]{2,1,0:T(8,128)S(1)} %dense.1.dense_ref, f32[24,256]{1,0:T(8,128)S(1)} %get-tuple-element.12.camera_ref), custom_call_target="tpu_custom_call" | custom-call | flops 10000000 | bytes 4000000 | tf_op jit(solution)/shard_map/return/pallas_call | solution.py:606
  (1 shorter events, 0.0 us)
Async XLA Ops:
  2.0 13.9 %all-to-all-start = ((s32[16,1,256]{2,1,0:T(1,128)}), s32[16,1,256]{2,1,0:T(1,128)S(1)}, u32[]{:S(2)}, u32[]{:S(2)}) async-start(s32[16,1,256]{2,1,0:T(1,128)} %all_to_all.13), calls=%async_computation | async-start | bytes 32768 | tf_op jit(solution)/shard_map/all_to_all | solution.py:555
  9.3 1.2 %copy-start = (f32[59,4096]{1,0:T(8,128)S(1)}, f32[59,4096]{1,0:T(8,128)}, u32[]{:S(2)}) copy-start(f32[59,4096]{1,0:T(8,128)} %params_ref.1) | copy-start | bytes 2899972
  10.6 0.7 %copy-start.1 = (s32[16,256]{1,0:T(8,128)S(1)}, s32[16,256]{1,0:T(8,128)}, u32[]{:S(2)}) copy-start(s32[16,256]{1,0:T(8,128)} %member_ref.3) | copy-start | bytes 49156
  10.6 0.8 %copy-start.2 = (f32[16,3,256]{2,0,1:T(8,128)S(1)}, f32[16,3,256]{2,0,1:T(8,128)}, u32[]{:S(2)}) copy-start(f32[16,3,256]{2,0,1:T(8,128)} %param.13) | copy-start | bytes 147460
  10.6 0.8 %copy-start.3 = (f32[3,8]{1,0:T(4,128)S(1)}, f32[3,8]{1,0:T(4,128)}, u32[]{:S(2)}) copy-start(f32[3,8]{1,0:T(4,128)} %cam_ref.1) | copy-start | bytes 292
  10.9 0.7 %copy-start.4 = (s32[16]{0:T(128)S(1)}, s32[16]{0:T(128)}, u32[]{:S(2)}) copy-start(s32[16]{0:T(128)} %length_ref.1) | copy-start | bytes 196
  10.9 0.7 %copy-start.5 = (s32[16]{0:T(128)S(1)}, s32[16]{0:T(128)}, u32[]{:S(2)}) copy-start(s32[16]{0:T(128)} %place_ref.1) | copy-start | bytes 196

commit v4 on v3

--- a/solution.py
+++ b/solution.py
@@ -249,14 +249,16 @@
     for axis in range(3):
         for k in range(views):
             row = axis * views + k
-            camera_ref[row : row + 1, :] = jnp.full((1, WIDE), cam_ref[axis, k], f32)
+            camera_ref[row : row + 1, :] = jnp.broadcast_to(cam_ref[axis : axis + 1, k : k + 1], (1, WIDE))
     wide = [(length_ref[t] > WIDE // 2).astype(i32) for t in range(tiles)]
     many = sum(wide[1:], wide[0])
     first, last = jnp.int32(0), many
     for t in range(tiles):
         plan_ref[jnp.where(wide[t] > 0, first, last)] = t
         first, last = first + wide[t], last + 1 - wide[t]
-    plan_ref[tiles] = lax.div(many + GROUP - 1, GROUP)
+    whole = lax.div(many + GROUP // 2 - 1, GROUP)
+    plan_ref[tiles] = whole
+    plan_ref[tiles + 1] = lax.div(many + GROUP - 1, GROUP)
 
     invert(member_ref, inverse_ref)
 
@@ -405,7 +407,8 @@
     rest = -0.5 * (lift * m + tilt * n) + jnp.log2(opacity)
     terms = [a, b, c, lift, tilt]
     terms = [jnp.where(live, term, 0.0) for term in terms] + [jnp.where(live, rest, FAR)]
-    coefs[...] = jnp.zeros_like(coefs)
+    for row in [*range(18, 32), *range(41, 48)]:
+        put(coefs, row * tiles, tiles, jnp.zeros((tiles, WIDE), f32))
     for k, term in enumerate(terms):
         for s, part in enumerate(pieces(term, 3)):
             row = 6 * s + k
@@ -436,13 +439,11 @@
 
     def some_tiles(turn, many):
         ts = [plan_ref[GROUP * turn + k] for k in range(GROUP)]
-        block = [pl.ds(pl.multiple_of(16 * t, 16), 16) for t in ts]
-        coef = [get(coefs, t, 32, tiles, many).astype(bf16) for t in ts]
-        color = [get(coefs, t + 32 * tiles, 16, tiles, many).astype(bf16) for t in ts]
+        coef = [get(coefs, t, 32, tiles, n).astype(bf16) for t, n in zip(ts, many)]
+        color = [get(coefs, t + 32 * tiles, 16, tiles, n).astype(bf16) for t, n in zip(ts, many)]
         alpha = [jnp.minimum(jnp.exp2(dot(monomials[...], x)), 0.99) for x in coef]
         parts = [pieces(jnp.log2(1.0 - x), 2) for x in alpha]
-        before = upper[:many, :many]
-        through = [jnp.exp2(stacked(high, low, before)) for high, low in parts]
+        through = [jnp.exp2(stacked(high, low, upper[:n, :n])) for (high, low), n in zip(parts, many)]
         weight = [x * y for x, y in zip(alpha, through)]
         parts = [pieces(x, 2) for x in weight]
         for t, x, (high, low) in zip(ts, color, parts):
@@ -456,25 +457,24 @@
             put(sums, pl.multiple_of(16 * t + 8, 8), 8, tint[0:8] + pltpu.roll(tint[0:8], 5, 0))
         pulled = [dot(turned_ref[t], x) * y for t, x, y in zip(ts, color, weight)]
         parts = [pieces(x, 2) for x in pulled]
-        after = lower[:many, :many]
-        behind = [stacked(high, low, after) for high, low in parts]
+        behind = [stacked(high, low, lower[:n, :n]) for (high, low), n in zip(parts, many)]
         for k, t in enumerate(ts):
             slope = pulled[k] - behind[k] * (alpha[k] / (1.0 - alpha[k]))
             high, low = pieces(jnp.where(alpha[k] < 0.99, slope, 0.0), 2)
             moment = dot(jnp.concatenate([moments[...]] * 2, axis=1), jnp.concatenate([high, low], axis=0))
             put(sums, pl.multiple_of(16 * t, 16), 8, moment[0:8])
 
-    def wide_turn(turn, carry):
-        some_tiles(turn, WIDE)
-        return carry
-
-    def narrow_turn(turn, carry):
-        some_tiles(turn, WIDE // 2)
-        return carry
-
-    wide_turns = plan_ref[tiles]
-    lax.fori_loop(0, wide_turns, wide_turn, 0)
-    lax.fori_loop(wide_turns, tiles // GROUP, narrow_turn, 0)
+    def turns(first, last, *many):
+        def one_turn(turn, carry):
+            some_tiles(turn, many)
+            return carry
+
+        lax.fori_loop(first, last, one_turn, 0)
+
+    wide, mixed = plan_ref[tiles], plan_ref[tiles + 1]
+    turns(0, wide, *[WIDE] * GROUP)
+    turns(wide, mixed, *[WIDE] * (GROUP // 2), *[WIDE // 2] * (GROUP // 2))
+    turns(mixed, tiles // GROUP, *[WIDE // 2] * GROUP)
     send = pltpu.make_async_copy(image, image_ref, sent)
     send.start()
 
@@ -558,14 +558,14 @@
     inverse, light, turned, centre, camera, plan = call(
         prepare_kernel,
         "prepare",
-        vmem(2) + smem(3),
+        vmem(2) + smem(2) + vmem(1),
         [
             index,
             shape(16 * tiles, WIDE, dtype=bf16),
             shape(tiles, WIDE, 16, dtype=bf16),
             shape(3, tiles, WIDE),
             shape(3 * cam_shift.shape[1], WIDE),
-            shape(tiles + 1, dtype=i32),
+            shape(tiles + 2, dtype=i32),
         ],
         [
             pltpu.VMEM((16 * tiles, WIDE), f32),

time: 51.8 us -> 51.2 us (0.988)
  Pallas kernels: 14.9 us -> 14.1 us
    pallas_call x1, Pallas kernels: 8.25 us -> 7.55 us  [on_device(): call(functools.partial(render_kernel, packed), 'render', vmem(6) + smem(1...]
where the time goes in v4:
time: 51.2 us; the launch traced here: 50.7 us
  blocking collectives  22.8 us (45%)
  Pallas kernels  14.1 us (28%)
  starting transfers between devices  7.36 us (14%)
  local copies, waits for them, and re-layouts  3.22 us (6%)
  waiting for transfers between devices  2.43 us (5%)
  between operations  0.7 us (1%)
    all_to_all x2, blocking collectives, travel(): parts = lax.all_to_all(parts, 'gs', split_axis=0, concat_axis=0, tiled=True)  22.8 us
    pallas_call x1, Pallas kernels, on_device(): call(functools.partial(render_kernel, packed), 'render', vmem(6) + smem(1...  7.55 us
    all_to_all x1, starting transfers between devices, on_device(): lax.all_to_all(requests, 'gs', split_axis=0, concat_axis=0, tiled=True)  7.36 us
    all_to_all x1, waiting for transfers between devices, on_device(): lax.all_to_all(requests, 'gs', split_axis=0, concat_axis=0, tiled=True)  2.43 us
    pallas_call x1, Pallas kernels, on_device(): call(functools.partial(return_kernel, slots, packed), 'return', vmem(4),...  2.32 us
    pallas_call x1, Pallas kernels, on_device(): call(functools.partial(owner_kernel, slots, packed), 'owner', vmem(3), [r...  2.13 us
    unnamed x13, local copies, waits for them, and re-layouts  1.89 us
    pallas_call x1, Pallas kernels, on_device(): call(prepare_kernel, 'prepare', vmem(2) + smem(2) + vmem(1), [index, shap...  1.84 us
  transfers between devices with their start and end apart: 1, of which 1 were waited for; matrix products, arithmetic and copies ran while one was open for 0% of the time, Pallas kernels for 4%

profile of v4, /device:TPU:0, one launch (start us, length us, event | category | flops | bytes accessed | tf_op | source)
XLA Modules:
  0.0 50.7 jit_solution(9015646689730463935)
XLA Ops:
  0.6 1.3 %all_to_all.13 = s32[16,1,256]{2,1,0:T(1,128)} reshape(s32[16,256]{1,0:T(8,128)} %param.8) | data formatting | bytes 32768 | tf_op jit(solution)/shard_map/all_to_all | solution.py:555
  2.0 7.4 %all-to-all-start = ((s32[16,1,256]{2,1,0:T(1,128)}), s32[16,1,256]{2,1,0:T(1,128)S(1)}, u32[]{:S(2)}, u32[]{:S(2)}) async-start(s32[16,1,256]{2,1,0:T(1,128)} %all_to_all.13), calls=%async_computation | async-start | bytes 32768 | tf_op jit(solution)/shard_map/all_to_all | solution.py:555
  9.3 0.0 copy-start
  9.3 1.2 %copy-done = f32[59,4096]{1,0:T(8,128)S(1)} copy-done((f32[59,4096]{1,0:T(8,128)S(1)}, f32[59,4096]{1,0:T(8,128)}, u32[]{:S(2)}) %copy-start) | copy-done | bytes 966680
  10.6 0.0 copy-start.1
  10.6 0.0 copy-start.2
  10.6 0.0 copy-start.3
  10.6 0.3 dense.1.dense_ref
  10.9 0.0 copy-start.4
  10.9 0.0 copy-start.5
  10.9 0.4 copy-done.1
  11.3 0.1 copy-done.2
  11.4 0.0 copy-done.3
  11.4 0.2 copy-done.4
  11.5 0.0 copy-done.5
  11.5 1.8 %prepare.1 = (s32[16,256]{1,0:T(8,128)S(1)}, bf16[256,256]{1,0:T(8,128)(2,1)S(1)}, bf16[16,256,16]{2,1,0:T(8,128)(2,1)S(1)}, f32[3,16,256]{2,1,0:T(8,128)S(1)}, f32[24,256]{1,0:T(8,128)S(1)}, /*index=5*/s32[18]{0:T(128)S(1)}) custom-call(s32[16,256]{1,0:T(8,128)S(1)} %copy-done.1, f32[3,16,256]{2,1,0:T(8,128)S(1)} %bitcast.14, s32[16]{0:T(128)S(1)} %copy-done.4, ...), custom_call_target="tpu_custom_call" | custom-call | flops 10000000 | bytes 4000000 | tf_op jit(solution)/shard_map/prepare/pallas_call | solution.py:558
  13.4 2.4 %all-to-all-done = s32[16,1,256]{2,1,0:T(1,128)S(1)} async-done(((s32[16,1,256]{2,1,0:T(1,128)}), s32[16,1,256]{2,1,0:T(1,128)S(1)}, u32[]{:S(2)}, u32[]{:S(2)}) %all-to-all-start) | async-done | bytes 16416 | tf_op jit(solution)/shard_map/all_to_all | solution.py:555
  15.8 2.1 %owner.1 = (f32[288,128]{1,0:T(8,128)S(1)}, s32[16,256]{1,0:T(8,128)S(1)}) custom-call(s32[16,256]{1,0:T(8,128)S(1)} %bitcast.13, f32[2,944,128]{2,1,0:T(8,128)S(1)} %dense.1.dense_ref, f32[24,256]{1,0:T(8,128)S(1)} %get-tuple-element.12.camera_ref), custom_call_target="tpu_custom_call" | custom-call | flops 10000000 | bytes 4000000 | tf_op jit(solution)/shard_map/owner/pallas_call | solution.py:576
  18.0 11.6 %all_to_all.21 = f32[16,1,2304]{2,1,0:T(1,128)S(1)} all-to-all(f32[16,1,2304]{2,1,0:T(1,128)S(1)} %bitcast.12), channel_id=1, replica_groups=mesh['groups'=2,'gs'=16] {'gs'}, dimensions={0} | all-to-all | bytes 294912 | tf_op jit(solution)/shard_map/all_to_all | solution.py:539
  29.6 7.6 %render.1 = (f32[3,16,256]{2,1,0:T(8,128)}, f32[288,128]{1,0:T(8,128)S(1)}) custom-call(f32[288,128]{1,0:T(8,128)S(1)} %bitcast.9, s32[16,256]{1,0:T(8,128)S(1)} %copy-done.1, s32[16,256]{1,0:T(8,128)S(1)} %get-tuple-element.14.inverse_ref, bf16[256,256]{1,0:T(8,128)(2,1)S(1)} %get-tuple-element.15.light_ref, ...), custom_call_target="tpu_custom_call" | custom-call | flops 100000000 | bytes 4000000 | tf_op jit(solution)/shard_map/render/pallas_call | solution.py:585
  37.1 11.2 %all_to_all.22 = f32[16,1,2304]{2,1,0:T(1,128)S(1)} all-to-all(f32[16,1,2304]{2,1,0:T(1,128)S(1)} %bitcast.11), channel_id=1, replica_groups=mesh['groups'=2,'gs'=16] {'gs'}, dimensions={0} | all-to-all | bytes 294912 | tf_op jit(solution)/shard_map/all_to_all | solution.py:539
  48.3 2.3 %return.1 = f32[59,4096]{1,0:T(8,128)} custom-call(f32[288,128]{1,0:T(8,128)S(1)} %bitcast.10, s32[16,256]{1,0:T(8,128)S(1)} %get-tuple-element.21.inverse_ref, f32[2,944,128]{2,1,0:T(8,128)S(1)} %dense.1.dense_ref, f32[24,256]{1,0:T(8,128)S(1)} %get-tuple-element.12.camera_ref), custom_call_target="tpu_custom_call" | custom-call | flops 10000000 | bytes 4000000 | tf_op jit(solution)/shard_map/return/pallas_call | solution.py:606
  (1 shorter events, 0.0 us)
Async XLA Ops:
  2.0 13.9 %all-to-all-start = ((s32[16,1,256]{2,1,0:T(1,128)}), s32[16,1,256]{2,1,0:T(1,128)S(1)}, u32[]{:S(2)}, u32[]{:S(2)}) async-start(s32[16,1,256]{2,1,0:T(1,128)} %all_to_all.13), calls=%async_computation | async-start | bytes 32768 | tf_op jit(solution)/shard_map/all_to_all | solution.py:555
  9.3 1.2 %copy-start = (f32[59,4096]{1,0:T(8,128)S(1)}, f32[59,4096]{1,0:T(8,128)}, u32[]{:S(2)}) copy-start(f32[59,4096]{1,0:T(8,128)} %params_ref.1) | copy-start | bytes 2899972
  10.6 0.7 %copy-start.1 = (s32[16,256]{1,0:T(8,128)S(1)}, s32[16,256]{1,0:T(8,128)}, u32[]{:S(2)}) copy-start(s32[16,256]{1,0:T(8,128)} %member_ref.3) | copy-start | bytes 49156
  10.6 0.8 %copy-start.2 = (f32[16,3,256]{2,0,1:T(8,128)S(1)}, f32[16,3,256]{2,0,1:T(8,128)}, u32[]{:S(2)}) copy-start(f32[16,3,256]{2,0,1:T(8,128)} %param.13) | copy-start | bytes 147460
  10.6 0.8 %copy-start.3 = (f32[3,8]{1,0:T(4,128)S(1)}, f32[3,8]{1,0:T(4,128)}, u32[]{:S(2)}) copy-start(f32[3,8]{1,0:T(4,128)} %cam_ref.1) | copy-start | bytes 292
  10.9 0.7 %copy-start.4 = (s32[16]{0:T(128)S(1)}, s32[16]{0:T(128)}, u32[]{:S(2)}) copy-start(s32[16]{0:T(128)} %length_ref.1) | copy-start | bytes 196
  10.9 0.7 %copy-start.5 = (s32[16]{0:T(128)S(1)}, s32[16]{0:T(128)}, u32[]{:S(2)}) copy-start(s32[16]{0:T(128)} %place_ref.1) | copy-start | bytes 196

commit v5 on v4

--- a/solution.py
+++ b/solution.py
@@ -290,9 +290,8 @@
     return [get(ref, k * blocks, blocks) for k in range(count)]
 
 
-def owner_kernel(slots_per, packed, asked_ref, dense_ref, camera_ref, attrs_ref, inverse_ref, held):
+def owner_kernel(slots_per, packed, width, asked_ref, dense_ref, camera_ref, attrs_ref, inverse_ref, held):
     blocks = asked_ref.shape[0]
-    width = dense_ref.shape[1] // blocks
     invert(asked_ref, inverse_ref)
     shift = shifts(inverse_ref[...], slots_per, camera_ref)
     table = dense_rows(dense_ref, width, blocks)
@@ -305,7 +304,7 @@
 
 def return_kernel(slots_per, packed, back_ref, inverse_ref, dense_ref, camera_ref, out_far, held, flat, grads, out_ref, sent):
     blocks = inverse_ref.shape[0]
-    width = dense_ref.shape[1] // blocks
+    width = out_far.shape[0]
     half = blocks // 2
     take_travel(back_ref, held, blocks, packed)
 
@@ -475,7 +474,7 @@
     turns(0, wide, *[WIDE] * GROUP)
     turns(wide, mixed, *[WIDE] * (GROUP // 2), *[WIDE // 2] * (GROUP // 2))
     turns(mixed, tiles // GROUP, *[WIDE // 2] * GROUP)
-    send = pltpu.make_async_copy(image, image_ref, sent)
+    send = pltpu.make_async_copy(image.at[:, pl.ds(0, tiles), :], image_ref, sent)
     send.start()
 
     m_xx, m_xy, m_yy, m_x, m_y, m_one = [get(sums, k, tiles, 16) for k in range(6)]
@@ -545,6 +544,7 @@
 def on_device(params, requests, member, tile_len, tile_pos, cam_shift, pixel_grad):
     peers, slots = requests.shape
     width, count = params.shape
+    tall = -(-width // 8) * 8
     tiles = member.shape[0]
     blocks = count // WIDE
     packed = slots % WIDE == 0
@@ -554,7 +554,7 @@
 
     asked = lax.all_to_all(requests, "gs", split_axis=0, concat_axis=0, tiled=True)
     asked = asked.reshape(blocks, WIDE)
-    (dense,) = call(dense_kernel, "dense", vmem(1), [shape(2, width * blocks, 128)], [], 1_000_000)(params)
+    (dense,) = call(dense_kernel, "dense", vmem(1), [shape(2, tall * blocks, 128)], [], 1_000_000)(params)
     inverse, light, turned, centre, camera, plan = call(
         prepare_kernel,
         "prepare",
@@ -574,7 +574,7 @@
         vmem(5) + smem(1),
     )(member, jnp.swapaxes(pixel_grad, 0, 1), tile_len, tile_pos, cam_shift)
     attrs, place = call(
-        functools.partial(owner_kernel, slots, packed),
+        functools.partial(owner_kernel, slots, packed, width),
         "owner",
         vmem(3),
         [rows, index],
@@ -588,7 +588,7 @@
         vmem(6) + smem(1),
         [shape(3, tiles, WIDE), rows],
         [
-            pltpu.VMEM((3, tiles, WIDE), f32),
+            pltpu.VMEM((3, tiles + 8, WIDE), f32),
             pltpu.SemaphoreType.DMA,
             held,
             held,
@@ -611,8 +611,8 @@
         [
             held,
             held,
-            pltpu.VMEM((2, width * blocks, 128), f32),
-            pltpu.VMEM((width, count), f32),
+            pltpu.VMEM((2, tall * blocks, 128), f32),
+            pltpu.VMEM((tall, count), f32),
             pltpu.SemaphoreType.DMA((2 * -(-width // 8),)),
         ],
         10_000_000,

time: 51.2 us -> 51.3 us (level)
  no operation moved by 1% of the time
where the time goes in v5:
time: 51.3 us; the launch traced here: 50.9 us
  blocking collectives  22.7 us (44%)
  Pallas kernels  14.5 us (28%)
  starting transfers between devices  7.36 us (14%)
  local copies, waits for them, and re-layouts  3.22 us (6%)
  waiting for transfers between devices  2.43 us (5%)
  between operations  0.7 us (1%)
    all_to_all x2, blocking collectives, travel(): parts = lax.all_to_all(parts, 'gs', split_axis=0, concat_axis=0, tiled=True)  22.7 us
    pallas_call x1, Pallas kernels, on_device(): call(functools.partial(render_kernel, packed), 'render', vmem(6) + smem(1...  7.91 us
    all_to_all x1, starting transfers between devices, on_device(): lax.all_to_all(requests, 'gs', split_axis=0, concat_axis=0, tiled=True)  7.36 us
    all_to_all x1, waiting for transfers between devices, on_device(): lax.all_to_all(requests, 'gs', split_axis=0, concat_axis=0, tiled=True)  2.43 us
    pallas_call x1, Pallas kernels, on_device(): call(functools.partial(return_kernel, slots, packed), 'return', vmem(4),...  2.33 us
    pallas_call x1, Pallas kernels, on_device(): call(functools.partial(owner_kernel, slots, packed, width), 'owner', vmem...  2.13 us
    unnamed x13, local copies, waits for them, and re-layouts  1.89 us
    pallas_call x1, Pallas kernels, on_device(): call(prepare_kernel, 'prepare', vmem(2) + smem(2) + vmem(1), [index, shap...  1.84 us
  transfers between devices with their start and end apart: 1, of which 1 were waited for; matrix products, arithmetic and copies ran while one was open for 0% of the time, Pallas kernels for 4%

profile of v5, /device:TPU:0, one launch (start us, length us, event | category | flops | bytes accessed | tf_op | source)
XLA Modules:
  0.0 50.9 jit_solution(17694204181638773804)
XLA Ops:
  0.6 1.3 %all_to_all.13 = s32[16,1,256]{2,1,0:T(1,128)} reshape(s32[16,256]{1,0:T(8,128)} %param.8) | data formatting | bytes 32768 | tf_op jit(solution)/shard_map/all_to_all | solution.py:555
  2.0 7.4 %all-to-all-start = ((s32[16,1,256]{2,1,0:T(1,128)}), s32[16,1,256]{2,1,0:T(1,128)S(1)}, u32[]{:S(2)}, u32[]{:S(2)}) async-start(s32[16,1,256]{2,1,0:T(1,128)} %all_to_all.13), calls=%async_computation | async-start | bytes 32768 | tf_op jit(solution)/shard_map/all_to_all | solution.py:555
  9.3 0.0 copy-start
  9.3 1.2 %copy-done = f32[59,4096]{1,0:T(8,128)S(1)} copy-done((f32[59,4096]{1,0:T(8,128)S(1)}, f32[59,4096]{1,0:T(8,128)}, u32[]{:S(2)}) %copy-start) | copy-done | bytes 966680
  10.6 0.0 copy-start.1
  10.6 0.0 copy-start.2
  10.6 0.0 copy-start.3
  10.6 0.3 dense.1.dense_ref
  10.9 0.0 copy-start.4
  10.9 0.0 copy-start.5
  10.9 0.4 copy-done.1
  11.3 0.1 copy-done.2
  11.4 0.0 copy-done.3
  11.4 0.2 copy-done.4
  11.5 0.0 copy-done.5
  11.5 1.8 %prepare.1 = (s32[16,256]{1,0:T(8,128)S(1)}, bf16[256,256]{1,0:T(8,128)(2,1)S(1)}, bf16[16,256,16]{2,1,0:T(8,128)(2,1)S(1)}, f32[3,16,256]{2,1,0:T(8,128)S(1)}, f32[24,256]{1,0:T(8,128)S(1)}, /*index=5*/s32[18]{0:T(128)S(1)}) custom-call(s32[16,256]{1,0:T(8,128)S(1)} %copy-done.1, f32[3,16,256]{2,1,0:T(8,128)S(1)} %bitcast.14, s32[16]{0:T(128)S(1)} %copy-done.4, ...), custom_call_target="tpu_custom_call" | custom-call | flops 10000000 | bytes 4000000 | tf_op jit(solution)/shard_map/prepare/pallas_call | solution.py:558
  13.4 2.4 %all-to-all-done = s32[16,1,256]{2,1,0:T(1,128)S(1)} async-done(((s32[16,1,256]{2,1,0:T(1,128)}), s32[16,1,256]{2,1,0:T(1,128)S(1)}, u32[]{:S(2)}, u32[]{:S(2)}) %all-to-all-start) | async-done | bytes 16416 | tf_op jit(solution)/shard_map/all_to_all | solution.py:555
  15.8 2.1 %owner.1 = (f32[288,128]{1,0:T(8,128)S(1)}, s32[16,256]{1,0:T(8,128)S(1)}) custom-call(s32[16,256]{1,0:T(8,128)S(1)} %bitcast.13, f32[2,1024,128]{2,1,0:T(8,128)S(1)} %dense.1.dense_ref, f32[24,256]{1,0:T(8,128)S(1)} %get-tuple-element.12.camera_ref), custom_call_target="tpu_custom_call" | custom-call | flops 10000000 | bytes 4000000 | tf_op jit(solution)/shard_map/owner/pallas_call | solution.py:576
  18.0 11.6 %all_to_all.21 = f32[16,1,2304]{2,1,0:T(1,128)S(1)} all-to-all(f32[16,1,2304]{2,1,0:T(1,128)S(1)} %bitcast.12), channel_id=1, replica_groups=mesh['groups'=2,'gs'=16] {'gs'}, dimensions={0} | all-to-all | bytes 294912 | tf_op jit(solution)/shard_map/all_to_all | solution.py:538
  29.6 7.9 %render.1 = (f32[3,16,256]{2,1,0:T(8,128)}, f32[288,128]{1,0:T(8,128)S(1)}) custom-call(f32[288,128]{1,0:T(8,128)S(1)} %bitcast.9, s32[16,256]{1,0:T(8,128)S(1)} %copy-done.1, s32[16,256]{1,0:T(8,128)S(1)} %get-tuple-element.14.inverse_ref, bf16[256,256]{1,0:T(8,128)(2,1)S(1)} %get-tuple-element.15.light_ref, ...), custom_call_target="tpu_custom_call" | custom-call | flops 100000000 | bytes 4000000 | tf_op jit(solution)/shard_map/render/pallas_call | solution.py:585
  37.5 11.1 %all_to_all.22 = f32[16,1,2304]{2,1,0:T(1,128)S(1)} all-to-all(f32[16,1,2304]{2,1,0:T(1,128)S(1)} %bitcast.11), channel_id=1, replica_groups=mesh['groups'=2,'gs'=16] {'gs'}, dimensions={0} | all-to-all | bytes 294912 | tf_op jit(solution)/shard_map/all_to_all | solution.py:538
  48.6 2.3 %return.1 = f32[59,4096]{1,0:T(8,128)} custom-call(f32[288,128]{1,0:T(8,128)S(1)} %bitcast.10, s32[16,256]{1,0:T(8,128)S(1)} %get-tuple-element.21.inverse_ref, f32[2,1024,128]{2,1,0:T(8,128)S(1)} %dense.1.dense_ref, f32[24,256]{1,0:T(8,128)S(1)} %get-tuple-element.12.camera_ref), custom_call_target="tpu_custom_call" | custom-call | flops 10000000 | bytes 4000000 | tf_op jit(solution)/shard_map/return/pallas_call | solution.py:606
  (1 shorter events, 0.0 us)
Async XLA Ops:
  2.0 13.9 %all-to-all-start = ((s32[16,1,256]{2,1,0:T(1,128)}), s32[16,1,256]{2,1,0:T(1,128)S(1)}, u32[]{:S(2)}, u32[]{:S(2)}) async-start(s32[16,1,256]{2,1,0:T(1,128)} %all_to_all.13), calls=%async_computation | async-start | bytes 32768 | tf_op jit(solution)/shard_map/all_to_all | solution.py:555
  9.3 1.2 %copy-start = (f32[59,4096]{1,0:T(8,128)S(1)}, f32[59,4096]{1,0:T(8,128)}, u32[]{:S(2)}) copy-start(f32[59,4096]{1,0:T(8,128)} %params_ref.1) | copy-start | bytes 2899972
  10.6 0.7 %copy-start.1 = (s32[16,256]{1,0:T(8,128)S(1)}, s32[16,256]{1,0:T(8,128)}, u32[]{:S(2)}) copy-start(s32[16,256]{1,0:T(8,128)} %member_ref.3) | copy-start | bytes 49156
  10.6 0.8 %copy-start.2 = (f32[16,3,256]{2,0,1:T(8,128)S(1)}, f32[16,3,256]{2,0,1:T(8,128)}, u32[]{:S(2)}) copy-start(f32[16,3,256]{2,0,1:T(8,128)} %param.13) | copy-start | bytes 147460
  10.6 0.8 %copy-start.3 = (f32[3,8]{1,0:T(4,128)S(1)}, f32[3,8]{1,0:T(4,128)}, u32[]{:S(2)}) copy-start(f32[3,8]{1,0:T(4,128)} %cam_ref.1) | copy-start | bytes 292
  10.9 0.7 %copy-start.4 = (s32[16]{0:T(128)S(1)}, s32[16]{0:T(128)}, u32[]{:S(2)}) copy-start(s32[16]{0:T(128)} %length_ref.1) | copy-start | bytes 196
  10.9 0.7 %copy-start.5 = (s32[16]{0:T(128)S(1)}, s32[16]{0:T(128)}, u32[]{:S(2)}) copy-start(s32[16]{0:T(128)} %place_ref.1) | copy-start | bytes 196
